TPU v7x, 32 devices: a whole 2x2x4 slice. The times are simulated.
32 devices in a mesh: grp: 2 (over x), ch: 16 (over z, y, core).
Axes of the slice: x: 2, y: 2, z: 4, core: 2. Of those that a mesh axis runs over, the one named last changes fastest.
Arguments:
- features: bfloat16 [2048, 2048], P('ch', 'grp'), parts along dimension 1, may hold values from -50 to 50
- dw_weight: float32 [2048, 49], P('ch'), may hold values from -0.875 to 0.875
- norm_gain: float32 [2048], replicated, may hold values from 0.25 to 1.75
- layer_scale: float32 [2048], replicated, may hold values from 0.2 to 1
- w_in: bfloat16 [8192, 2048], P('ch'), may hold values from -0.125 to 0.125
- w_out: bfloat16 [8192, 2048], P('ch'), may hold values from -0.0625 to 0.0625
- w_head: bfloat16 [2048, 150], replicated, may hold values from -3 to 3
- labels: int32 [2048], P('grp'), parts along dimension 0, may hold values from 0 to 149
Outputs:
- d_features: float32 [2048, 2048], P('ch', 'grp'), parts along dimension 1
- d_dw: float32 [2048, 98], P('ch', 'grp'), parts along dimension 1
- d_scale: float32 [4096], P(('grp', 'ch')), parts along dimension 0
- d_w_in: float32 [16384, 2048], P(('grp', 'ch')), parts along dimension 0
- d_w_out: float32 [16384, 2048], P(('grp', 'ch')), parts along dimension 0
- d_head: float32 [2048, 300], P('ch', 'grp'), parts along dimension 1
- mean_loss: float32 [2], P('grp'), parts along dimension 0
There are 2 independent parts, one for each index of `grp`. A program takes and returns all parts, laid end to end along the dimension named above; an argument that names none is the same for every part. Nothing has to cross between parts.
All inputs are finite; a program needn't handle non-finite values.
Results may differ from a plain program's by a relative error of at most 0.012.
Values may be sent and summed in bfloat16 or wider, within the bound.
A program may use at most 128 MiB of HBM per device.

v0:
```python
import functools
import jax
import jax.numpy as jnp
from jax import lax
from jax.experimental import pallas as pl
from jax.experimental.pallas import tpu as pltpu
from jax.sharding import PartitionSpec as P

KS = 7
WIN_H = 32
WIN_W = 32

norm_eps = 1e-06
VMEM_LIMIT = 56 * 1024 * 1024


def slide(values, rows, cols):
    area = values.shape[1]
    token = lax.broadcasted_iota(jnp.int32, values.shape, 1)
    step = rows * WIN_W + cols
    if step == 0:
        return values
    spot = (token & (WIN_W - 1)) if cols else token
    inside = (spot < (WIN_W if cols else area) - step) if step > 0 else (spot >= -step)
    return jnp.where(inside, pltpu.roll(values, (-step) % area, 1), 0.0)


def conv_rows(values, taps):
    half = KS // 2
    shifted = [slide(values, 0, j - half) for j in range(KS)]
    running = None
    for i in range(KS):
        line = sum(taps[:, i * KS + j : i * KS + j + 1] * shifted[j] for j in range(KS))
        line = slide(line, i - half, 0)
        running = line if running is None else running + line
    return running


def conv_back_kernel(grad_ref, x_ref, taps_ref, add_ref, dx_ref, dtaps_ref):
    half = KS // 2
    wide = dtaps_ref.shape[1]

    @pl.loop(0, x_ref.shape[0] // 8)
    def _(g):
        own = pl.ds(pl.multiple_of(g * 8, 8), 8)
        grad, values, taps = grad_ref[own, :], x_ref[own, :], taps_ref[own, :]
        lifted = [slide(grad, half - i, 0) for i in range(KS)]
        column = lax.broadcasted_iota(jnp.int32, (8, wide), 1)
        dtaps = jnp.zeros((8, wide), jnp.float32)
        dx = add_ref[own, :]
        for j in range(KS):
            line = sum(taps[:, i * KS + j : i * KS + j + 1] * lifted[i] for i in range(KS))
            dx = dx + slide(line, 0, half - j)
            shifted = slide(values, 0, j - half)
            for i in range(KS):
                whole = jnp.sum(lifted[i] * shifted, axis=1, keepdims=True)
                dtaps = jnp.where(column == i * KS + j, whole, dtaps)
        dx_ref[own, :] = dx
        dtaps_ref[own, :] = dtaps


def conv_back(grad, values, taps, add):
    return pl.pallas_call(
        conv_back_kernel,
        out_shape=(
            jax.ShapeDtypeStruct(grad.shape, jnp.float32),
            jax.ShapeDtypeStruct(taps.shape, jnp.float32),
        ),
        in_specs=[pl.BlockSpec(memory_space=pltpu.VMEM)] * 4,
        out_specs=(pl.BlockSpec(memory_space=pltpu.VMEM),) * 2,
        compiler_params=pltpu.CompilerParams(vmem_limit_bytes=32 * 1024 * 1024),
    )(grad, values, taps, add)


def gelu_parts(values):
    cum_prob = 0.5 * (1.0 + lax.erf(values * 0.7071067811865476))
    density = jnp.exp(-0.5 * values * values) * 0.3989422804014327
    return (values * cum_prob, cum_prob + values * density)


def place(n):
    me = lax.axis_index("ch")
    return lax.div(me, 4), lax.rem(lax.div(me, 2), 2), lax.rem(me, 2)


def index_of(z, y, c):
    return (z * 2 + y) * 2 + c


def greet(devices, z, a, between=None):
    barrier = pltpu.get_barrier_semaphore()
    for device in devices:
        pl.semaphore_signal(barrier, inc=1, device_id={"ch": device})
    me = lax.axis_index("ch")

    @pl.when(z > 0)
    def _():
        pl.semaphore_signal(barrier, inc=1, device_id={"ch": me - 4})

    @pl.when(z < a - 1)
    def _():
        pl.semaphore_signal(barrier, inc=1, device_id={"ch": me + 4})

    if between is not None:
        between()
    count = len(devices) + jnp.where(z > 0, 1, 0) + jnp.where(z < a - 1, 1, 0)
    pl.semaphore_wait(barrier, count)


def gather_kernel(
    n, x_ref, taps_ref, w_ref, head_ref, out_ref, mixed_ref, wide, conv, send_sem, recv_sem
):
    a = n // 4
    rows = x_ref.shape[0]
    parts = 2 if rows % 32 == 0 else 1
    chunk = rows // parts
    z, y, c = place(n)
    me = index_of(z, y, c)
    twin, across = index_of(z, y, 1 - c), index_of(z, 1 - y, c)

    def convolve():
        wide[...] = x_ref[...].astype(jnp.float32)

        convolve_part(0)

    def convolve_part(h):
        first = h * chunk

        @pl.loop(0, chunk // 8)
        def _(g):
            own = pl.ds(pl.multiple_of(first + g * 8, 8), 8)
            conv[own, :] = conv_rows(wide[own, :], taps_ref[own, :])

        out_ref[pl.ds(pl.multiple_of(me * rows + first, chunk), chunk)] = conv[
            first : first + chunk
        ].astype(jnp.bfloat16)

    greet([twin, across], z, a, convolve)

    def copy(kind, b, device, h):
        piece = out_ref.at[pl.ds(pl.multiple_of(b * rows + h * chunk, chunk), chunk)]
        return pltpu.make_async_remote_copy(
            src_ref=piece,
            dst_ref=piece,
            send_sem=send_sem.at[kind, b * parts + h],
            recv_sem=recv_sem.at[b * parts + h],
            device_id={"ch": device},
        )

    def send_own(h):
        @pl.when(z < a - 1)
        def _():
            copy(0, me, me + 4, h).start()

        @pl.when(z > 0)
        def _():
            copy(1, me, me - 4, h).start()

        copy(2, me, across, h).start()
        copy(3, me, twin, h).start()

    for h in range(parts):
        if h > 0:
            convolve_part(h)
        send_own(h)

    head = head_ref[...]
    high = head.astype(jnp.bfloat16)
    low = (head - high.astype(jnp.float32)).astype(jnp.bfloat16)
    units = w_ref.shape[0]
    part = min(units, 128)

    @pl.loop(0, units // part)
    def _(g):
        own = pl.ds(pl.multiple_of(g * part, part), part)
        weights = w_ref[own, :]
        mixed_ref[own, :] = jnp.dot(
            weights, high, preferred_element_type=jnp.float32
        ) + jnp.dot(weights, low, preferred_element_type=jnp.float32)

    def from_line(s, h):
        below, above = me - 4 * s, me + 4 * s

        @pl.when(z >= s)
        def _():
            copy(0, below, me, h).wait_recv()

            @pl.when(z < a - 1)
            def _():
                copy(0, below, me + 4, h).start()

            copy(2, below, across, h).start()
            copy(3, below, twin, h).start()

        @pl.when(z + s < a)
        def _():
            copy(1, above, me, h).wait_recv()

            @pl.when(z > 0)
            def _():
                copy(1, above, me - 4, h).start()

            copy(2, above, across, h).start()
            copy(3, above, twin, h).start()

    def from_across(s, h):
        def take(b):
            copy(2, b, across, h).wait_recv()
            copy(3, b, twin, h).start()

        if s == 0:
            take(across)
            return

        @pl.when(z >= s)
        def _():
            take(across - 4 * s)

        @pl.when(z + s < a)
        def _():
            take(across + 4 * s)

    for s in range(1, a):
        for h in range(parts):
            from_line(s, h)
            from_across(s - 1, h)
    for h in range(parts):
        from_across(a - 1, h)

    for h in range(parts):
        for q in range(n // 2):
            copy(3, q * 2 + 1 - c, twin, h).wait_recv()
            copy(3, q * 2 + c, twin, h).wait_send()
        for zz in range(a):
            copy(2, index_of(zz, y, c), across, h).wait_send()

            @pl.when((z < a - 1) & (zz <= z))
            def _():
                copy(0, index_of(zz, y, c), me + 4, h).wait_send()

            @pl.when((z > 0) & (zz >= z))
            def _():
                copy(1, index_of(zz, y, c), me - 4, h).wait_send()


def gather(n, x, taps, weights, head):
    rows, cols = x.shape
    return pl.pallas_call(
        functools.partial(gather_kernel, n),
        out_shape=(
            jax.ShapeDtypeStruct((n * rows, cols), x.dtype),
            jax.ShapeDtypeStruct((weights.shape[0], head.shape[1]), jnp.float32),
        ),
        in_specs=[pl.BlockSpec(memory_space=pltpu.VMEM)] * 4,
        out_specs=(pl.BlockSpec(memory_space=pltpu.VMEM),) * 2,
        scratch_shapes=[
            pltpu.VMEM((rows, cols), jnp.float32),
            pltpu.VMEM((rows, cols), jnp.float32),
            pltpu.SemaphoreType.DMA((4, 2 * n)),
            pltpu.SemaphoreType.DMA((2 * n,)),
        ],
        compiler_params=pltpu.CompilerParams(
            collective_id=0, has_side_effects=True, vmem_limit_bytes=VMEM_LIMIT
        ),
    )(x, taps, weights, head)


def total_kernel(n, x_ref, out_ref, buf, from_twin, acc, slots, sums, t_sem, r_sem, g_sem, f_sem):
    m = n // 2
    height, cols = x_ref.shape
    strips = cols // 128
    half = height * strips // 2
    rows = half // m
    me = lax.axis_index("ch")
    q, c = lax.div(me, 2), lax.rem(me, 2)
    twin = q * 2 + 1 - c
    barrier = pltpu.get_barrier_semaphore()
    pl.semaphore_signal(barrier, inc=1, device_id={"ch": twin})
    for d in range(1, m):
        pl.semaphore_signal(barrier, inc=1, device_id={"ch": lax.rem(q + d, m) * 2 + c})
    for j in range(strips):
        buf[j * height : (j + 1) * height, :] = x_ref[:, j * 128 : (j + 1) * 128]
    pl.semaphore_wait(barrier, m)

    def piece(ref, start, length):
        return ref.at[pl.ds(pl.multiple_of(start, 8), length)]

    swap = pltpu.make_async_remote_copy(
        src_ref=piece(buf, (1 - c) * half, half),
        dst_ref=from_twin,
        send_sem=t_sem.at[0],
        recv_sem=t_sem.at[1],
        device_id={"ch": twin},
    )
    swap.start()
    swap.wait_recv()
    acc[...] = buf[pl.ds(pl.multiple_of(c * half, 8), half), :] + from_twin[...]

    def scatter(d):
        other = lax.rem(q + d, m)
        return pltpu.make_async_remote_copy(
            src_ref=piece(acc, other * rows, rows),
            dst_ref=slots.at[d],
            send_sem=r_sem.at[0, d],
            recv_sem=r_sem.at[1, d],
            device_id={"ch": other * 2 + c},
        )

    for d in range(1, m):
        scatter(d).start()
    mine = acc[pl.ds(pl.multiple_of(q * rows, 8), rows), :]
    for d in range(1, m):
        scatter(d).wait_recv()
        mine = mine + slots[d]
    my_start = c * half + q * rows
    sums[pl.ds(pl.multiple_of(my_start, 8), rows), :] = mine

    def spread(d, start, device):
        return pltpu.make_async_remote_copy(
            src_ref=piece(sums, start, rows),
            dst_ref=piece(sums, start, rows),
            send_sem=g_sem.at[0, d],
            recv_sem=g_sem.at[1, d],
            device_id={"ch": device},
        )

    def forward(d, start):
        return pltpu.make_async_remote_copy(
            src_ref=piece(sums, start, rows),
            dst_ref=piece(sums, start, rows),
            send_sem=f_sem.at[0, d],
            recv_sem=f_sem.at[1, d],
            device_id={"ch": twin},
        )

    for d in range(1, m):
        spread(d, my_start, lax.rem(q + d, m) * 2 + c).start()
    forward(0, my_start).start()
    for d in range(1, m):
        start = c * half + lax.rem(q - d + m, m) * rows
        spread(d, start, twin).wait_recv()
        forward(d, start).start()
    for d in range(m):
        forward(d, (1 - c) * half + lax.rem(q - d + m, m) * rows).wait_recv()
    for j in range(strips):
        out_ref[:, j * 128 : (j + 1) * 128] = sums[j * height : (j + 1) * height, :]
    swap.wait_send()
    for d in range(1, m):
        scatter(d).wait_send()
        spread(d, my_start, twin).wait_send()
    for d in range(m):
        forward(d, my_start).wait_send()


def total(n, x):
    height, cols = x.shape
    area = height * (cols // 128)
    m = n // 2
    return pl.pallas_call(
        functools.partial(total_kernel, n),
        out_shape=jax.ShapeDtypeStruct(x.shape, x.dtype),
        in_specs=[pl.BlockSpec(memory_space=pltpu.VMEM)],
        out_specs=pl.BlockSpec(memory_space=pltpu.VMEM),
        scratch_shapes=[
            pltpu.VMEM((area, 128), jnp.float32),
            pltpu.VMEM((area // 2, 128), jnp.float32),
            pltpu.VMEM((area // 2, 128), jnp.float32),
            pltpu.VMEM((m, area // n, 128), jnp.float32),
            pltpu.VMEM((area, 128), jnp.float32),
            pltpu.SemaphoreType.DMA((2,)),
            pltpu.SemaphoreType.DMA((2, m)),
            pltpu.SemaphoreType.DMA((2, m)),
            pltpu.SemaphoreType.DMA((2, m)),
        ],
        compiler_params=pltpu.CompilerParams(
            collective_id=1, has_side_effects=True, vmem_limit_bytes=VMEM_LIMIT
        ),
    )(x)


def scatter_kernel(
    n, conv_ref, w_ref, p_ref, rows_ref, seen_ref, out_ref,
    g_ref, t_in, y_in, u_in, d_in, y_out, z_out, t_sem, y_sem, u_sem, d_sem, zs_sem
):
    a = n // 4
    rows = out_ref.shape[0]
    z, y, c = place(n)
    me = index_of(z, y, c)
    twin, across = index_of(z, y, 1 - c), index_of(z, 1 - y, c)
    greet([twin, across], z, a)

    def own(b):
        return pl.ds(pl.multiple_of(b * rows, rows), rows)

    def order(k):
        if k == a - 1:
            return z
        low = jnp.where(k < a - 1 - z, a - 1 - k, k - (a - 1 - z))
        high = jnp.where(k < z, k, a - 1 - (k - z))
        return jnp.where(2 * z < a, low, high)

    def to_twin(zz, side, core):
        return pltpu.make_async_remote_copy(
            src_ref=g_ref.at[own(index_of(zz, side, core))],
            dst_ref=t_in.at[zz * 2 + side],
            send_sem=t_sem.at[0, zz * 2 + side],
            recv_sem=t_sem.at[1, zz * 2 + side],
            device_id={"ch": twin},
        )

    def to_across(k, zz):
        return pltpu.make_async_remote_copy(
            src_ref=y_out.at[k],
            dst_ref=y_in.at[zz],
            send_sem=y_sem.at[0, zz],
            recv_sem=y_sem.at[1, zz],
            device_id={"ch": across},
        )

    def along(k, zz, landing, sem, device):
        return pltpu.make_async_remote_copy(
            src_ref=z_out.at[k],
            dst_ref=landing.at[zz],
            send_sem=zs_sem.at[k],
            recv_sem=sem.at[zz],
            device_id={"ch": device},
        )

    tokens = conv_ref.shape[1]
    tok_mean, inv_std = rows_ref[0:1, :], rows_ref[1:2, :]
    mean_gained, mean_both = rows_ref[2:3, :], rows_ref[3:4, :]

    def fill(zz, side, core):
        mine = own(index_of(zz, side, core))
        grad = jnp.dot(w_ref[mine, :], p_ref[...], preferred_element_type=jnp.float32)
        normed = (conv_ref[mine, :].astype(jnp.float32) - tok_mean) * inv_std
        term = (grad - mean_gained - normed * mean_both) * inv_std
        g_ref[mine, :tokens] = term.astype(jnp.bfloat16)
        g_ref[mine, tokens:] = seen_ref[mine, :]

    def cross(k):
        zz = order(k)
        to_twin(zz, 1 - y, c).wait_recv()
        y_out[k] = (
            g_ref[own(index_of(zz, 1 - y, c))].astype(jnp.float32)
            + t_in[zz * 2 + 1 - y].astype(jnp.float32)
        ).astype(jnp.bfloat16)
        to_across(k, zz).start()

    for k in range(a):
        fill(order(k), 1 - y, 1 - c)
        to_twin(order(k), 1 - y, 1 - c).start()
        fill(order(k), 1 - y, c)
        if k > 0:
            cross(k - 1)
    fill(order(0), y, 1 - c)
    to_twin(order(0), y, 1 - c).start()
    cross(a - 1)
    fill(order(0), y, c)
    for k in range(a):
        zz = order(k)
        if k < a - 1:
            fill(order(k + 1), y, 1 - c)
            to_twin(order(k + 1), y, 1 - c).start()
            fill(order(k + 1), y, c)
        to_twin(zz, y, c).wait_recv()
        to_across(k, zz).wait_recv()
        term = (
            g_ref[own(index_of(zz, y, c))].astype(jnp.float32)
            + t_in[zz * 2 + y].astype(jnp.float32)
            + y_in[zz].astype(jnp.float32)
        )
        if k < a - 1:
            out_ref[...] = term

            @pl.when((zz > z) & (z > 0))
            def _():
                along(k, zz, u_in, u_sem, me).wait_recv()
                out_ref[...] += u_in[zz].astype(jnp.float32)

            @pl.when((zz < z) & (z < a - 1))
            def _():
                along(k, zz, d_in, d_sem, me).wait_recv()
                out_ref[...] += d_in[zz].astype(jnp.float32)

            z_out[k] = out_ref[...].astype(jnp.bfloat16)

            @pl.when(zz > z)
            def _():
                along(k, zz, u_in, u_sem, me + 4).start()

            @pl.when(zz < z)
            def _():
                along(k, zz, d_in, d_sem, me - 4).start()

        else:
            out_ref[...] = term

            @pl.when(z > 0)
            def _():
                along(0, z, u_in, u_sem, me).wait_recv()
                out_ref[...] += u_in[z].astype(jnp.float32)

            @pl.when(z < a - 1)
            def _():
                along(0, z, d_in, d_sem, me).wait_recv()
                out_ref[...] += d_in[z].astype(jnp.float32)

    for k in range(a):
        zz = order(k)
        to_twin(zz, 1 - y, 1 - c).wait_send()
        to_twin(zz, y, 1 - c).wait_send()
        to_across(k, zz).wait_send()
        if k < a - 1:
            along(k, zz, u_in, u_sem, me).wait_send()


def scatter(n, conv_all, weights, pre_grad, token_rows, seen):
    rows, cols = conv_all.shape[0] // n, conv_all.shape[1] + seen.shape[1]
    a = n // 4
    return pl.pallas_call(
        functools.partial(scatter_kernel, n),
        out_shape=jax.ShapeDtypeStruct((rows, cols), jnp.float32),
        in_specs=[pl.BlockSpec(memory_space=pltpu.VMEM)] * 5,
        out_specs=pl.BlockSpec(memory_space=pltpu.VMEM),
        scratch_shapes=[
            pltpu.VMEM((n * rows, cols), jnp.bfloat16),
            pltpu.VMEM((n // 2, rows, cols), jnp.bfloat16),
            pltpu.VMEM((a, rows, cols), jnp.bfloat16),
            pltpu.VMEM((a, rows, cols), jnp.bfloat16),
            pltpu.VMEM((a, rows, cols), jnp.bfloat16),
            pltpu.VMEM((a, rows, cols), jnp.bfloat16),
            pltpu.VMEM((a, rows, cols), jnp.bfloat16),
            pltpu.SemaphoreType.DMA((2, n // 2)),
            pltpu.SemaphoreType.DMA((2, a)),
            pltpu.SemaphoreType.DMA((a,)),
            pltpu.SemaphoreType.DMA((a,)),
            pltpu.SemaphoreType.DMA((a,)),
        ],
        compiler_params=pltpu.CompilerParams(
            collective_id=2, has_side_effects=True, vmem_limit_bytes=VMEM_LIMIT
        ),
    )(conv_all, weights, pre_grad, token_rows, seen)


def dot(lhs, rhs, over, precision=None):
    return lax.dot_general(
        lhs, rhs, ((over[:1], over[1:]), ((), ())),
        precision=precision, preferred_element_type=jnp.float32,
    )


def per_device(n, features, dw_weight, norm_gain, layer_scale, w_in, w_out, w_head, labels):
    fine = lax.Precision.HIGH
    my_rows, tok_count = features.shape
    channels, class_count = w_head.shape
    row_offset = lax.axis_index("ch") * my_rows
    inputs_wide = features.astype(jnp.float32)
    classes = -(-class_count // max(n, 16)) * max(n, 16)
    head_pad = jnp.pad(w_head, ((0, 0), (0, classes - class_count)))
    scaled_head = layer_scale[:, None] * head_pad.astype(jnp.float32)
    conv_all, mixed = gather(n, features, dw_weight, w_out, scaled_head)
    conv_wide = conv_all.astype(jnp.float32)
    tok_mean = jnp.mean(conv_wide, axis=0)
    centered = conv_wide - tok_mean[None, :]
    tok_var = jnp.mean(centered * centered, axis=0)
    inv_std = 1.0 / jnp.sqrt(tok_var + norm_eps)
    norm_out = (norm_gain[:, None] * (centered * inv_std[None, :])).astype(jnp.bfloat16)
    pre_act = jnp.dot(w_in, norm_out, preferred_element_type=jnp.float32)
    gelu_out, gelu_slope = gelu_parts(pre_act)
    hidden = gelu_out.astype(jnp.bfloat16)

    my_scale = lax.dynamic_slice_in_dim(layer_scale, row_offset, my_rows, 0)
    my_head = lax.dynamic_slice_in_dim(head_pad, row_offset, my_rows, 0)
    my_head_wide = my_head.astype(jnp.float32)
    part = dot(mixed, hidden.astype(jnp.float32), (0, 0), fine) + dot(my_head, features, (0, 0))
    logits = total(n, part)

    kinds = lax.broadcasted_iota(jnp.int32, (classes, tok_count), 0)
    logits = jnp.where(kinds < class_count, logits, -jnp.inf)
    row_max = jnp.max(logits, axis=0, keepdims=True)
    exp_terms = jnp.exp(logits - row_max)
    exp_total = jnp.sum(exp_terms, axis=0, keepdims=True)
    log_total = jnp.log(exp_total) + row_max
    hit = kinds == labels[None, :]
    picked = jnp.sum(jnp.where(hit, logits, 0.0), axis=0)
    mean_loss = jnp.mean(log_total[0] - picked).reshape(1)
    logit_grad = exp_terms / exp_total - hit.astype(jnp.float32)
    grad_narrow = logit_grad.astype(jnp.bfloat16)

    out_grad = dot(my_head_wide, logit_grad, (1, 0), fine)
    seen = dot(hidden, grad_narrow, (1, 1))
    hidden_grad = dot(mixed, logit_grad, (1, 0), fine)
    seen_narrow = seen.astype(jnp.bfloat16)
    d_w_out = dot(seen_narrow, scaled_head.astype(jnp.bfloat16), (1, 1))
    branch_seen = dot(w_out, seen_narrow, (0, 0)).astype(jnp.bfloat16)
    pre_grad_wide = hidden_grad * gelu_slope
    pre_grad = pre_grad_wide.astype(jnp.bfloat16)
    d_w_in = dot(pre_grad, norm_out, (1, 1))
    gain_rows = jnp.sum(w_in.astype(jnp.float32) * norm_gain[None, :], axis=1)
    mean_gained = jnp.sum(gain_rows[:, None] * pre_grad_wide, axis=0) / channels
    mean_both = jnp.sum(pre_act * pre_grad_wide, axis=0) / channels
    weights = (w_in.astype(jnp.float32) * norm_gain[None, :]).astype(jnp.bfloat16).T
    width = -(-classes // 128) * 128
    token_rows = jnp.stack([tok_mean, inv_std, mean_gained, mean_both])
    token_rows = jnp.pad(token_rows, ((0, 4), (0, 0)))
    branch_seen = jnp.pad(branch_seen, ((0, 0), (0, width - classes)))
    landed = scatter(n, conv_all, weights, pre_grad, token_rows, branch_seen)
    conv_grad = landed[:, :tok_count]
    my_seen = landed[:, tok_count : tok_count + class_count]
    d_head = dot(inputs_wide, logit_grad, (1, 1), fine)[:, :class_count] + my_scale[:, None] * my_seen
    d_scale = jnp.sum(my_head_wide[:, :class_count] * my_seen, axis=1)
    d_features, d_dw = conv_back(conv_grad, inputs_wide, dw_weight, out_grad)
    return (d_features, d_dw, d_scale, d_w_in, d_w_out, d_head, mean_loss)


def solution(mesh):
    placed = (P("ch", "grp"), P("ch", None), P(), P(), P("ch", None), P("ch", None), P(), P("grp"))
    return jax.shard_map(
        functools.partial(per_device, mesh.shape["ch"]),
        mesh=mesh,
        in_specs=placed,
        out_specs=(
            P("ch", "grp"),
            P("ch", "grp"),
            P(("grp", "ch")),
            P(("grp", "ch"), None),
            P(("grp", "ch"), None),
            P("ch", "grp"),
            P("grp"),
        ),
        check_vma=False,
    )
```

profile of v0, /device:TPU:0, one launch (start us, length us, event | category | flops | bytes accessed | tf_op | source)
XLA Modules:
  0.0 169.2 jit_solution(17507642800510824985)
XLA Ops:
  0.6 1.5 copy.24.taps_ref
  2.1 1.4 copy.23
  3.5 2.4 %convert_multiply_fusion.1.head_ref = f32[2048,160]{1,0:T(8,128)} fusion(f32[2048]{0:T(1024)} %param.11, bf16[2048,150]{1,0:T(8,128)(2,1)S(1)} %copy.23), kind=kLoop, calls=%fused_computation.27 | loop fusion | flops 655360 | bytes 1933312 | tf_op jit(solution)/shard_map/mul | solution.py:561
  5.9 37.9 %shard_map.135 = (bf16[2048,1024]{1,0:T(8,128)(2,1)}, f32[512,160]{1,0:T(8,128)}) custom-call(bf16[128,1024]{1,0:T(8,128)(2,1)} %x_ref.1, f32[128,49]{1,0:T(8,128)} %copy.24.taps_ref, bf16[512,2048]{1,0:T(8,128)(2,1)} %w_ref.1, f32[2048,160]{1,0:T(8,128)} %convert_multiply_fusion.1.head_ref), custom_call_target="tpu_custom_call" | custom-call | tf_op jit(solution)/shard_map/pallas_call | solution.py:248
  43.7 0.0 copy-start.16
  43.8 2.9 %copy.25 = bf16[512,2048]{0,1:T(8,128)(2,1)S(1)} copy(bf16[512,2048]{1,0:T(8,128)(2,1)} %param.12) | data formatting | bytes 4194304 | tf_op args[4]
  46.6 0.0 copy-done.16
  46.6 0.0 copy-start.1
  46.6 2.4 %fusion.5 = (f32[512]{0:T(512)}, bf16[2048,512]{1,0:T(8,128)(2,1)}) fusion(bf16[512,2048]{0,1:T(8,128)(2,1)S(1)} %copy.25, f32[2048]{0:T(1024)S(1)} %copy-done.16), kind=kLoop, calls=%fused_computation.8 | loop fusion | flops 4193792 | bytes 4204544 | tf_op jit(solution)/shard_map/reduce_sum | solution.py:600
  49.1 0.5 copy-done.1
  49.6 0.7 convert_reduce_fusion
  50.3 1.2 fusion.2
  51.5 0.4 copy-done.7
  51.9 3.8 %fusion.16 = (bf16[512,1024]{1,0:T(8,128)(2,1)S(1)}, f32[1024,512]{0,1:T(8,128)}) fusion(bf16[512,2048]{1,0:T(8,128)(2,1)S(1)} %copy-done.7, bf16[2048,1024]{1,0:T(8,128)(2,1)S(1)} %copy-done.1, f32[1024]{0:T(1024)S(1)} %add_rsqrt_fusion, f32[1024]{0:T(1024)S(1)} %broadcast_multiply_fusion.2, f32[2048]{0:T(1024)S(1)} %copy-done.16), kind=kOutput, calls=%fused_computation.24 | convolution fusion | flops 2160590848 | bytes 9453568 | tf_op jit(solution)/shard_map/dot_general | solution.py:569
  55.7 0.0 copy-done.13
  55.7 0.0 copy-done.11
  55.7 0.6 fusion.27
  56.3 0.4 copy-done.5
  56.6 1.1 convolution_add_fusion.x_ref
  57.8 23.2 %shard_map.136 = f32[160,1024]{1,0:T(8,128)} custom-call(f32[160,1024]{1,0:T(8,128)} %convolution_add_fusion.x_ref), custom_call_target="tpu_custom_call" | custom-call | tf_op jit(solution)/shard_map/pallas_call | solution.py:359
  81.0 0.0 copy-start.21
  81.0 1.2 select_reduce_fusion.1
  82.2 0.0 copy-done.18
  82.2 1.3 select_reduce_fusion
  83.6 0.0 copy-done.20
  83.6 0.0 copy-done.23
  83.6 0.0 copy-start.14
  83.6 0.0 copy-start.4
  83.6 4.4 %multiply_reduce_fusion = (f32[1024]{0:T(1024)S(1)}, f32[1024]{0:T(1024)S(1)}, bf16[512,1024]{1,0:T(8,128)(2,1)}) fusion(f32[512]{0:T(512)S(1)} %copy-done.20, f32[1024,512]{0,1:T(8,128)S(1)} %copy-done.23, f32[512,160]{1,0:T(8,128)S(1)} %copy-done.11, f32[160,1024]{1,0:T(8,128)} %shard_map.136, s32[1024]{0:T(1024)S(1)} %copy-done.18, ...), kind=kOutput, calls=%fused_computation.26 | convolution fusion | flops 511637504 | bytes 4151456 | tf_op jit(solution)/shard_map/dot_general | solution.py:547
  88.0 0.0 copy-done.14
  88.0 0.6 select_maximum_fusion.rows_ref
  88.6 0.0 copy-done.21
  88.6 0.0 copy-done.4
  88.6 0.6 convolution_convert_fusion.1
  89.2 0.0 copy-start.9
  89.2 0.7 copy-done.9
  89.9 0.4 copy-done.3
  90.3 0.5 convolution_convert_fusion
  90.8 0.7 copy.26
  91.5 1.2 pad.14.seen_ref
  92.7 44.1 %shard_map.137 = f32[128,1280]{1,0:T(8,128)} custom-call(bf16[2048,1024]{1,0:T(8,128)(2,1)} %get-tuple-element.11.conv_ref, bf16[2048,512]{1,0:T(8,128)(2,1)} %get-tuple-element.34.w_ref, bf16[512,1024]{1,0:T(8,128)(2,1)} %get-tuple-element.35.p_ref, f32[8,1024]{1,0:T(8,128)} %select_maximum_fusion.rows_ref, bf16[2048,256]{1,0:T(8,128)(2,1)} %pad.14.seen_ref), custom_call_target="tpu_custom_call" | custom-call | tf_op jit(solution)/shard_map/pallas_call | solution.py:521
  136.7 1.1 slice.15.grad_ref
  137.8 0.0 copy-done.6
  137.8 0.0 copy-start
  137.9 0.0 copy-done.19
  137.9 0.0 copy-done.22
  137.9 0.6 fusion.26.add_ref
  138.5 0.2 copy-done
  138.7 16.5 %shard_map.138 = (f32[128,1024]{1,0:T(8,128)}, f32[128,49]{1,0:T(8,128)S(1)}) custom-call(f32[128,1024]{1,0:T(8,128)S(1)} %slice.15.grad_ref, f32[128,1024]{1,0:T(8,128)S(1)} %convert_element_type.63.x_ref, f32[128,49]{1,0:T(8,128)S(1)} %copy-done, f32[128,1024]{1,0:T(8,128)S(1)} %fusion.26.add_ref), custom_call_target="tpu_custom_call" | custom-call | tf_op jit(solution)/shard_map/pallas_call | solution.py:63
  155.2 0.7 copy.29
  155.9 0.5 convolution_bitcast_fusion
  156.4 0.0 copy-done.12
  156.5 0.1 dynamic_slice.7
  156.5 1.8 %slice_add_fusion = (f32[128,150]{1,0:T(8,128)S(1)}, f32[128]{0:T(128)}) fusion(f32[128,160]{1,0:T(8,128)S(1)} %convolution_bitcast_fusion, f32[128,1280]{1,0:T(8,128)} %shard_map.137, f32[128]{0:T(128)S(1)} %dynamic_slice.7, s32[]{:T(128)S(6)} %select_n.11, bf16[2048,150]{1,0:T(8,128)(2,1)S(1)} %copy.23), kind=kLoop, calls=%fused_computation.44 | loop fusion | flops 95872 | bytes 845828 | tf_op jit(solution)/shard_map/add | solution.py:611
  158.4 0.0 copy-done.8
  158.4 0.0 copy-done.2
  158.4 0.0 copy-done.15
  158.4 0.0 copy-done.17
  158.4 0.0 copy-start.10
  158.4 4.6 %fusion.20 = f32[512,2048]{1,0:T(8,128)} fusion(bf16[512,1024]{1,0:T(8,128)(2,1)S(1)} %copy-done.8, bf16[2048,1024]{1,0:T(8,128)(2,1)S(1)} %copy-done.2, f32[1024]{0:T(1024)S(1)} %copy-done.15, f32[1024]{0:T(1024)S(1)} %broadcast_multiply_fusion.2, f32[2048]{0:T(1024)S(1)} %copy-done.17), kind=kOutput, calls=%fused_computation.35 | convolution fusion | flops 2157969408 | bytes 9453568 | tf_op jit(solution)/shard_map/dot_general | solution.py:547
  163.0 0.0 copy-done.10
  163.0 3.1 %fusion.18 = f32[512,2048]{1,0:T(8,128)} fusion(bf16[512,160]{0,1:T(8,128)(2,1)S(1)} %copy-done.10, f32[2048]{0:T(1024)S(1)} %copy-done.12, bf16[2048,150]{1,0:T(8,128)(2,1)S(1)} %copy.23), kind=kOutput, calls=%fused_computation.31 | convolution fusion | flops 336527360 | bytes 4980736 | tf_op jit(solution)/shard_map/dot_general | solution.py:547
  166.1 0.7 copy.30
  166.8 0.6 subtract_reduce_fusion
  (21 shorter events, 0.1 us)
Async XLA Ops:
  43.7 2.9 %copy-start.16 = (f32[2048]{0:T(1024)S(1)}, f32[2048]{0:T(1024)}, u32[]{:S(2)}) copy-start(f32[2048]{0:T(1024)} %param.10) | copy-start | bytes 24580
  46.6 2.9 %copy-start.1 = (bf16[2048,1024]{1,0:T(8,128)(2,1)S(1)}, bf16[2048,1024]{1,0:T(8,128)(2,1)}, u32[]{:S(2)}) copy-start(bf16[2048,1024]{1,0:T(8,128)(2,1)} %get-tuple-element.11.conv_ref) | copy-start | bytes 12582916
  50.3 1.6 copy-start.7
  51.9 3.8 %copy-start.13 = (f32[1024]{0:T(1024)}, f32[1024]{0:T(1024)S(1)}, u32[]{:S(2)}) copy-start(f32[1024]{0:T(1024)S(1)} %add_rsqrt_fusion) | copy-start | bytes 12292
  51.9 3.8 %copy-start.11 = (f32[512,160]{1,0:T(8,128)S(1)}, f32[512,160]{1,0:T(8,128)}, u32[]{:S(2)}) copy-start(f32[512,160]{1,0:T(8,128)} %get-tuple-element.12) | copy-start | bytes 983044
  55.7 1.0 copy-start.5
  56.6 25.6 %copy-start.18 = (s32[1024]{0:T(1024)S(1)}, s32[1024]{0:T(1024)}, u32[]{:S(2)}) copy-start(s32[1024]{0:T(1024)} %param.15) | copy-start | bytes 12292
  56.6 26.9 %copy-start.20 = (f32[512]{0:T(512)S(1)}, f32[512]{0:T(512)}, u32[]{:S(2)}) copy-start(f32[512]{0:T(512)} %get-tuple-element.33) | copy-start | bytes 6148
  56.6 26.9 %copy-start.23 = (f32[1024,512]{0,1:T(8,128)S(1)}, f32[1024,512]{0,1:T(8,128)}, u32[]{:S(2)}) copy-start(f32[1024,512]{0,1:T(8,128)} %get-tuple-element.39) | copy-start | bytes 6291460
  81.0 7.7 %copy-start.21 = (pred[160]{0:T(512)(128)(4,1)}, pred[160]{0:T(512)(128)(4,1)S(1)}, u32[]{:S(2)}) copy-start(pred[160]{0:T(512)(128)(4,1)S(1)} %iota_compare_fusion.2) | copy-start | bytes 484
  83.6 4.4 %copy-start.14 = (f32[1024]{0:T(1024)S(1)}, f32[1024]{0:T(1024)}, u32[]{:S(2)}) copy-start(f32[1024]{0:T(1024)} %copy-done.13) | copy-start | bytes 12292
  83.6 5.0 %copy-start.4 = (f32[160,1024]{1,0:T(8,128)S(1)}, f32[160,1024]{1,0:T(8,128)}, u32[]{:S(2)}) copy-start(f32[160,1024]{1,0:T(8,128)} %shard_map.136) | copy-start | bytes 1966084
  88.6 1.7 copy-start.3
  89.2 0.7 copy-start.9
  92.7 45.2 %copy-start.6 = (bf16[128,1024]{1,0:T(8,128)(2,1)S(1)}, bf16[128,1024]{1,0:T(8,128)(2,1)}, u32[]{:S(2)}) copy-start(bf16[128,1024]{1,0:T(8,128)(2,1)} %x_ref.1) | copy-start | bytes 786436
  92.7 45.3 %copy-start.19 = (s32[1024]{0:T(1024)S(1)}, s32[1024]{0:T(1024)}, u32[]{:S(2)}) copy-start(s32[1024]{0:T(1024)} %param.15) | copy-start | bytes 12292
  92.7 45.3 %copy-start.22 = (pred[160]{0:T(512)(128)(4,1)S(1)}, pred[160]{0:T(512)(128)(4,1)}, u32[]{:S(2)}) copy-start(pred[160]{0:T(512)(128)(4,1)} %copy-done.21) | copy-start | bytes 484
  137.8 0.8 copy-start
  138.7 19.7 %copy-start.8 = (bf16[512,1024]{1,0:T(8,128)(2,1)S(1)}, bf16[512,1024]{1,0:T(8,128)(2,1)}, u32[]{:S(2)}) copy-start(bf16[512,1024]{1,0:T(8,128)(2,1)} %get-tuple-element.35.p_ref) | copy-start | bytes 3145732
  155.2 1.2 copy-start.12
  155.9 2.5 %copy-start.2 = (bf16[2048,1024]{1,0:T(8,128)(2,1)S(1)}, bf16[2048,1024]{1,0:T(8,128)(2,1)}, u32[]{:S(2)}) copy-start(bf16[2048,1024]{1,0:T(8,128)(2,1)} %get-tuple-element.11.conv_ref) | copy-start | bytes 12582916
  155.9 2.5 %copy-start.15 = (f32[1024]{0:T(1024)S(1)}, f32[1024]{0:T(1024)}, u32[]{:S(2)}) copy-start(f32[1024]{0:T(1024)} %copy-done.13) | copy-start | bytes 12292
  155.9 2.5 %copy-start.17 = (f32[2048]{0:T(1024)S(1)}, f32[2048]{0:T(1024)}, u32[]{:S(2)}) copy-start(f32[2048]{0:T(1024)} %param.10) | copy-start | bytes 24580
  158.4 4.6 %copy-start.10 = (bf16[512,160]{0,1:T(8,128)(2,1)S(1)}, bf16[512,160]{0,1:T(8,128)(2,1)}, u32[]{:S(2)}) copy-start(bf16[512,160]{0,1:T(8,128)(2,1)} %copy-done.9) | copy-start | bytes 491524
where the time goes:
time: 170 us; the launch traced here: 169 us
  Pallas kernels  122 us (72%)
  matrix products  19.7 us (12%)
  local copies, waits for them, and re-layouts  12.8 us (8%)
  other arithmetic  12.4 us (7%)
  between operations  2.7 us (2%)
    pallas_call x1, Pallas kernels, scatter(): pl.pallas_call(functools.partial(scatter_kernel, n), out_shape=jax.ShapeD...  44.1 us
    pallas_call x1, Pallas kernels, gather(): pl.pallas_call(functools.partial(gather_kernel, n), out_shape=(jax.ShapeD...  37.9 us
    pallas_call x1, Pallas kernels, total(): pl.pallas_call(functools.partial(total_kernel, n), out_shape=jax.ShapeDty...  23.2 us
    pallas_call x1, Pallas kernels, conv_back(): pl.pallas_call(conv_back_kernel, out_shape=(jax.ShapeDtypeStruct(grad.sha...  16.5 us
    dot_general x9, matrix products, dot(): lax.dot_general(lhs, rhs, ((over[:1], over[1:]), ((), ())), precision=pre...  15.9 us
    unnamed x53, local copies, waits for them, and re-layouts  9.78 us
    dot_general x1, matrix products, per_device(): pre_act = jnp.dot(w_in, norm_out, preferred_element_type=jnp.float32)  3.81 us

commit v1 on v0

--- a/solution.py
+++ b/solution.py
@@ -34,42 +34,6 @@
         line = slide(line, i - half, 0)
         running = line if running is None else running + line
     return running
-
-
-def conv_back_kernel(grad_ref, x_ref, taps_ref, add_ref, dx_ref, dtaps_ref):
-    half = KS // 2
-    wide = dtaps_ref.shape[1]
-
-    @pl.loop(0, x_ref.shape[0] // 8)
-    def _(g):
-        own = pl.ds(pl.multiple_of(g * 8, 8), 8)
-        grad, values, taps = grad_ref[own, :], x_ref[own, :], taps_ref[own, :]
-        lifted = [slide(grad, half - i, 0) for i in range(KS)]
-        column = lax.broadcasted_iota(jnp.int32, (8, wide), 1)
-        dtaps = jnp.zeros((8, wide), jnp.float32)
-        dx = add_ref[own, :]
-        for j in range(KS):
-            line = sum(taps[:, i * KS + j : i * KS + j + 1] * lifted[i] for i in range(KS))
-            dx = dx + slide(line, 0, half - j)
-            shifted = slide(values, 0, j - half)
-            for i in range(KS):
-                whole = jnp.sum(lifted[i] * shifted, axis=1, keepdims=True)
-                dtaps = jnp.where(column == i * KS + j, whole, dtaps)
-        dx_ref[own, :] = dx
-        dtaps_ref[own, :] = dtaps
-
-
-def conv_back(grad, values, taps, add):
-    return pl.pallas_call(
-        conv_back_kernel,
-        out_shape=(
-            jax.ShapeDtypeStruct(grad.shape, jnp.float32),
-            jax.ShapeDtypeStruct(taps.shape, jnp.float32),
-        ),
-        in_specs=[pl.BlockSpec(memory_space=pltpu.VMEM)] * 4,
-        out_specs=(pl.BlockSpec(memory_space=pltpu.VMEM),) * 2,
-        compiler_params=pltpu.CompilerParams(vmem_limit_bytes=32 * 1024 * 1024),
-    )(grad, values, taps, add)
 
 
 def gelu_parts(values):
@@ -543,6 +507,152 @@
     )(conv_all, weights, pre_grad, token_rows, seen)
 
 
+LANES = 128
+SUB = 8
+PAD_W = WIN_W + 16
+
+
+def fit(value, axis, length):
+    short = length - value.shape[axis]
+    if short == 0:
+        return value
+    pads = [(0, 0)] * value.ndim
+    pads[axis] = (0, short)
+    return jnp.pad(value, pads)
+
+
+def clear_pads(grid_ref):
+    half = KS // 2
+    blank = jnp.zeros((half, PAD_W, LANES), jnp.float32)
+    grid_ref[0:half] = blank
+    grid_ref[half + WIN_H : 2 * half + WIN_H] = blank
+
+    @pl.loop(0, WIN_H)
+    def _(h):
+        edge = jnp.zeros((SUB, LANES), jnp.float32)
+        grid_ref[half + h, 0:SUB, :] = edge
+        grid_ref[half + h, SUB + WIN_W : PAD_W, :] = edge
+
+
+def put_strip(grid_ref, strip, block):
+    half = KS // 2
+    turned = block.T
+    for r in range(LANES // WIN_W):
+        grid_ref[half + strip * (LANES // WIN_W) + r, SUB : SUB + WIN_W, :] = turned[
+            r * WIN_W : (r + 1) * WIN_W
+        ]
+
+
+def spread_taps(taps_ref, wide_ref):
+    for k in range(KS * KS):
+        wide_ref[k] = jnp.broadcast_to(taps_ref[k : k + 1, :], (SUB, LANES))
+
+
+ROWS_AT_ONCE = 8
+
+
+def conv_piece(grid_ref, taps_ref, first, col, flip=False):
+    outs = [None] * ROWS_AT_ONCE
+    for j in range(KS):
+        start = SUB + col + j - KS // 2
+        seen = [
+            grid_ref[first + r, start : start + SUB, :] for r in range(ROWS_AT_ONCE + KS - 1)
+        ]
+        for i in range(KS):
+            k = i * KS + j
+            tap = taps_ref[KS * KS - 1 - k if flip else k]
+            for r in range(ROWS_AT_ONCE):
+                term = tap * seen[r + i]
+                outs[r] = term if outs[r] is None else outs[r] + term
+    return outs
+
+
+def tail_kernel(
+    x_ref, grad_ref, taps_ref, lg_ref, head_ref, seen_ref, scale_ref,
+    dx_ref, dtaps_ref, dscale_ref, dhead_ref,
+    x_grid, g_grid, turned, wide, taps, sums
+):
+    rows, tokens = x_ref.shape
+    strips = tokens // LANES
+    wide[...] = jnp.zeros_like(wide)
+    wide[0:rows, :] = x_ref[...].astype(jnp.float32)
+    spread_taps(taps_ref, taps)
+    clear_pads(x_grid)
+    clear_pads(g_grid)
+    for s in range(strips):
+        put_strip(x_grid, s, wide[:, s * LANES : (s + 1) * LANES])
+        put_strip(g_grid, s, grad_ref[:, s * LANES : (s + 1) * LANES])
+    sums[...] = jnp.zeros_like(sums)
+    half = KS // 2
+
+    @pl.loop(0, WIN_H // ROWS_AT_ONCE)
+    def _(block):
+        first = block * ROWS_AT_ONCE
+        for col in range(0, WIN_W, SUB):
+            outs = conv_piece(g_grid, taps, first, col, flip=True)
+            for r in range(ROWS_AT_ONCE):
+                turned[first + r, col : col + SUB, :] = outs[r]
+            grads = [
+                g_grid[first + half + r, SUB + col : SUB + col + SUB, :]
+                for r in range(ROWS_AT_ONCE)
+            ]
+            for j in range(KS):
+                start = SUB + col + j - half
+                seen = [
+                    x_grid[first + r, start : start + SUB, :]
+                    for r in range(ROWS_AT_ONCE + KS - 1)
+                ]
+                for i in range(KS):
+                    total = sums[i * KS + j]
+                    for r in range(ROWS_AT_ONCE):
+                        total = total + grads[r] * seen[r + i]
+                    sums[i * KS + j] = total
+
+    for k in range(KS * KS):
+        dtaps_ref[k : k + 1, :] = jnp.sum(sums[k], axis=0, keepdims=True)
+
+    head = head_ref[...].astype(jnp.float32).T.astype(jnp.bfloat16)
+    per = LANES // WIN_W
+    for s in range(strips):
+        own = slice(s * LANES, (s + 1) * LANES)
+        back = jnp.concatenate([turned[s * per + r] for r in range(per)], axis=0).T
+        out_grad = jnp.dot(head, lg_ref[:, own], preferred_element_type=jnp.float32)
+        dx_ref[:, own] = (back + out_grad)[0:rows]
+    direct = lax.dot_general(
+        lg_ref[...], wide[...].astype(jnp.bfloat16), (((1,), (1,)), ((), ())),
+        preferred_element_type=jnp.float32,
+    )
+    seen = seen_ref[...]
+    classes = dhead_ref.shape[0]
+    dhead_ref[...] = (direct + scale_ref[...] * seen)[0:classes]
+    dscale_ref[...] = jnp.sum(head_ref[...].astype(jnp.float32) * seen, axis=0, keepdims=True)
+
+
+def tail(classes, x, grad, taps, lg, head, seen, scale):
+    rows, tokens = x.shape
+    vmem = pl.BlockSpec(memory_space=pltpu.VMEM)
+    return pl.pallas_call(
+        tail_kernel,
+        out_shape=(
+            jax.ShapeDtypeStruct((rows, tokens), jnp.float32),
+            jax.ShapeDtypeStruct((KS * KS, LANES), jnp.float32),
+            jax.ShapeDtypeStruct((1, LANES), jnp.float32),
+            jax.ShapeDtypeStruct((classes, LANES), jnp.float32),
+        ),
+        in_specs=[vmem] * 7,
+        out_specs=(vmem,) * 4,
+        scratch_shapes=[
+            pltpu.VMEM((WIN_H + KS - 1, PAD_W, LANES), jnp.float32),
+            pltpu.VMEM((WIN_H + KS - 1, PAD_W, LANES), jnp.float32),
+            pltpu.VMEM((WIN_H, WIN_W, LANES), jnp.float32),
+            pltpu.VMEM((LANES, tokens), jnp.float32),
+            pltpu.VMEM((KS * KS, SUB, LANES), jnp.float32),
+            pltpu.VMEM((KS * KS, SUB, LANES), jnp.float32),
+        ],
+        compiler_params=pltpu.CompilerParams(vmem_limit_bytes=VMEM_LIMIT),
+    )(x, grad, taps, lg, head, seen, scale)
+
+
 def dot(lhs, rhs, over, precision=None):
     return lax.dot_general(
         lhs, rhs, ((over[:1], over[1:]), ((), ())),
@@ -555,7 +665,6 @@
     my_rows, tok_count = features.shape
     channels, class_count = w_head.shape
     row_offset = lax.axis_index("ch") * my_rows
-    inputs_wide = features.astype(jnp.float32)
     classes = -(-class_count // max(n, 16)) * max(n, 16)
     head_pad = jnp.pad(w_head, ((0, 0), (0, classes - class_count)))
     scaled_head = layer_scale[:, None] * head_pad.astype(jnp.float32)
@@ -572,7 +681,6 @@
 
     my_scale = lax.dynamic_slice_in_dim(layer_scale, row_offset, my_rows, 0)
     my_head = lax.dynamic_slice_in_dim(head_pad, row_offset, my_rows, 0)
-    my_head_wide = my_head.astype(jnp.float32)
     part = dot(mixed, hidden.astype(jnp.float32), (0, 0), fine) + dot(my_head, features, (0, 0))
     logits = total(n, part)
 
@@ -588,7 +696,6 @@
     logit_grad = exp_terms / exp_total - hit.astype(jnp.float32)
     grad_narrow = logit_grad.astype(jnp.bfloat16)
 
-    out_grad = dot(my_head_wide, logit_grad, (1, 0), fine)
     seen = dot(hidden, grad_narrow, (1, 1))
     hidden_grad = dot(mixed, logit_grad, (1, 0), fine)
     seen_narrow = seen.astype(jnp.bfloat16)
@@ -606,11 +713,16 @@
     token_rows = jnp.pad(token_rows, ((0, 4), (0, 0)))
     branch_seen = jnp.pad(branch_seen, ((0, 0), (0, width - classes)))
     landed = scatter(n, conv_all, weights, pre_grad, token_rows, branch_seen)
-    conv_grad = landed[:, :tok_count]
-    my_seen = landed[:, tok_count : tok_count + class_count]
-    d_head = dot(inputs_wide, logit_grad, (1, 1), fine)[:, :class_count] + my_scale[:, None] * my_seen
-    d_scale = jnp.sum(my_head_wide[:, :class_count] * my_seen, axis=1)
-    d_features, d_dw = conv_back(conv_grad, inputs_wide, dw_weight, out_grad)
+    conv_grad = fit(landed[:, :tok_count], 0, LANES)
+    my_seen = fit(landed[:, tok_count : tok_count + classes].T, 1, LANES)
+    own_head = fit(my_head.T, 1, LANES)
+    d_features, d_dw, d_scale, d_head = tail(
+        class_count, features, conv_grad, fit(dw_weight.T, 1, LANES), grad_narrow, own_head, my_seen,
+        fit(my_scale[None, :], 1, LANES),
+    )
+    d_dw = d_dw.T[:my_rows]
+    d_scale = d_scale[0, :my_rows]
+    d_head = d_head.T[:my_rows]
     return (d_features, d_dw, d_scale, d_w_in, d_w_out, d_head, mean_loss)
 
 

time: 170 us -> 159 us (0.935)
  Pallas kernels: 122 us -> 112 us
  other arithmetic: 12.4 us -> 9 us
  local copies, waits for them, and re-layouts: 12.8 us -> 15 us
    pallas_call x1, Pallas kernels: 16.5 us -> 6.48 us  [tail(): pl.pallas_call(tail_kernel, out_shape=(jax.ShapeDtypeStruct((rows, tokens...]
    unnamed x53 -> x29, local copies, waits for them, and re-layouts: 9.78 us -> 7.35 us
    add x1 -> x0, other arithmetic: 1.85 us -> none  [per_device(): dot(inputs_wide, logit_grad, (1, 1), fine)[:, :class_count]]
    slice x1 -> x2, local copies, waits for them, and re-layouts: 1.08 us -> 2.89 us  [the longest x1 1.97 us: per_device(): conv_grad = fit(landed[:, :tok_count], 0, LANES)]
    mul x0 -> x1, local copies, waits for them, and re-layouts: none -> 1.77 us  [per_device(): scaled_head = layer_scale[:, None] * head_pad.astype(jnp.float32)]
    dot_general x9 -> x7, matrix products: 15.9 us -> 16.4 us  [dot(): lax.dot_general(lhs, rhs, ((over[:1], over[1:]), ((), ())), precision=pre...]
where the time goes in v1:
time: 159 us
  Pallas kernels  112 us (70%)
  matrix products  20.3 us (13%)
  local copies, waits for them, and re-layouts  15 us (9%)
  other arithmetic  9 us (6%)
  between operations  2.62 us (2%)
    pallas_call x1, Pallas kernels, scatter(): pl.pallas_call(functools.partial(scatter_kernel, n), out_shape=jax.ShapeD...  44.1 us
    pallas_call x1, Pallas kernels, gather(): pl.pallas_call(functools.partial(gather_kernel, n), out_shape=(jax.ShapeD...  37.9 us
    pallas_call x1, Pallas kernels, total(): pl.pallas_call(functools.partial(total_kernel, n), out_shape=jax.ShapeDty...  23.2 us
    dot_general x7, matrix products, dot(): lax.dot_general(lhs, rhs, ((over[:1], over[1:]), ((), ())), precision=pre...  16.4 us
    unnamed x29, local copies, waits for them, and re-layouts  7.35 us
    pallas_call x1, Pallas kernels, tail(): pl.pallas_call(tail_kernel, out_shape=(jax.ShapeDtypeStruct((rows, tokens...  6.48 us
    dot_general x1, matrix products, per_device(): pre_act = jnp.dot(w_in, norm_out, preferred_element_type=jnp.float32)  3.82 us

profile of v1, /device:TPU:0, one launch (start us, length us, event | category | flops | bytes accessed | tf_op | source)
XLA Modules:
  0.0 158.6 jit_solution(13027735530968817937)
XLA Ops:
  0.6 1.5 copy.20.taps_ref
  2.1 1.2 convert_multiply_fusion.1
  3.3 1.8 %copy.21.head_ref = f32[2048,160]{1,0:T(8,128)} copy(f32[2048,160]{0,1:T(8,128)S(1)} %convert_multiply_fusion.1) | data formatting | bytes 2621440 | tf_op jit(solution)/shard_map/mul | solution.py:670
  5.1 37.9 %shard_map.135 = (bf16[2048,1024]{1,0:T(8,128)(2,1)}, f32[512,160]{1,0:T(8,128)}) custom-call(bf16[128,1024]{1,0:T(8,128)(2,1)} %x_ref.3, f32[128,49]{1,0:T(8,128)} %copy.20.taps_ref, bf16[512,2048]{1,0:T(8,128)(2,1)} %w_ref.1, f32[2048,160]{1,0:T(8,128)} %copy.21.head_ref), custom_call_target="tpu_custom_call" | custom-call | tf_op jit(solution)/shard_map/pallas_call | solution.py:212
  43.0 0.0 copy-start.11
  43.0 2.9 %copy.22 = bf16[512,2048]{0,1:T(8,128)(2,1)S(1)} copy(bf16[512,2048]{1,0:T(8,128)(2,1)} %param.12) | data formatting | bytes 4194304 | tf_op args[4]
  45.9 0.0 copy-done.11
  45.9 0.0 copy-start
  45.9 1.9 %fusion.5 = (f32[512]{0:T(512)S(1)}, bf16[2048,512]{1,0:T(8,128)(2,1)}) fusion(bf16[512,2048]{0,1:T(8,128)(2,1)S(1)} %copy.22, f32[2048]{0:T(1024)S(1)} %copy-done.11), kind=kLoop, calls=%fused_computation.8 | loop fusion | flops 4193792 | bytes 4204544 | tf_op jit(solution)/shard_map/reduce_sum | solution.py:707
  47.8 1.1 copy-done
  48.8 0.7 convert_reduce_fusion
  49.5 0.0 copy-start.6
  49.5 1.2 fusion.2
  50.7 0.4 copy-done.6
  51.1 0.0 copy-start.8
  51.1 3.8 %fusion.16 = (bf16[512,1024]{1,0:T(8,128)(2,1)S(1)}, f32[1024,512]{0,1:T(8,128)}) fusion(bf16[512,2048]{1,0:T(8,128)(2,1)S(1)} %copy-done.6, bf16[2048,1024]{1,0:T(8,128)(2,1)S(1)} %copy-done, f32[1024]{0:T(1024)S(1)} %add_rsqrt_fusion, f32[1024]{0:T(1024)S(1)} %broadcast_multiply_fusion.2, f32[2048]{0:T(1024)S(1)} %copy-done.11), kind=kOutput, calls=%fused_computation.24 | convolution fusion | flops 2160590848 | bytes 9453568 | tf_op jit(solution)/shard_map/dot_general | solution.py:678
  54.9 0.0 copy-start.2
  54.9 0.0 copy-start.5
  54.9 0.0 copy-done.8
  54.9 0.6 fusion.28
  55.5 0.0 copy-start.10
  55.5 0.5 copy-done.2
  56.0 0.1 copy-done.5
  56.1 0.0 copy-start.12
  56.1 1.1 convolution_add_fusion.x_ref
  57.2 23.2 %shard_map.136 = f32[160,1024]{1,0:T(8,128)} custom-call(f32[160,1024]{1,0:T(8,128)} %convolution_add_fusion.x_ref), custom_call_target="tpu_custom_call" | custom-call | tf_op jit(solution)/shard_map/pallas_call | solution.py:323
  80.4 1.2 select_reduce_fusion.1
  81.6 0.0 copy-done.10
  81.6 1.3 select_reduce_fusion
  82.9 0.0 copy-done.12
  83.0 0.0 copy-start.1
  83.0 4.3 %multiply_reduce_fusion = (f32[1024]{0:T(1024)S(1)}, f32[1024]{0:T(1024)S(1)}, bf16[512,1024]{1,0:T(8,128)(2,1)}) fusion(f32[512]{0:T(512)S(1)} %get-tuple-element.23, f32[1024,512]{0,1:T(8,128)S(1)} %copy-done.12, f32[512,160]{1,0:T(8,128)S(1)} %copy-done.8, f32[160,1024]{1,0:T(8,128)} %shard_map.136, s32[1024]{0:T(1024)S(1)} %copy-done.10, ...), kind=kOutput, calls=%fused_computation.26 | convolution fusion | flops 511637504 | bytes 4151456 | tf_op jit(solution)/shard_map/dot_general | solution.py:657
  87.3 0.0 copy-start.3
  87.3 0.6 select_maximum_fusion.rows_ref
  88.0 0.0 copy-done.1
  88.0 0.2 fusion.27.lg_ref
  88.2 0.0 copy-start.4
  88.2 0.5 convolution_convert_fusion.1
  88.7 0.2 copy-done.3
  88.9 0.5 convolution_convert_fusion
  89.4 0.0 copy-done.4
  89.5 0.7 copy.23
  90.1 1.1 pad.14.seen_ref
  91.3 44.1 %shard_map.137 = f32[128,1280]{1,0:T(8,128)} custom-call(bf16[2048,1024]{1,0:T(8,128)(2,1)} %get-tuple-element.13.conv_ref, bf16[2048,512]{1,0:T(8,128)(2,1)} %get-tuple-element.24.w_ref, bf16[512,1024]{1,0:T(8,128)(2,1)} %get-tuple-element.25.p_ref, f32[8,1024]{1,0:T(8,128)} %select_maximum_fusion.rows_ref, bf16[2048,256]{1,0:T(8,128)(2,1)} %pad.14.seen_ref), custom_call_target="tpu_custom_call" | custom-call | tf_op jit(solution)/shard_map/pallas_call | solution.py:485
  135.4 0.0 copy-start.9
  135.4 0.0 copy-start.7
  135.4 2.0 %slice.6.grad_ref = f32[128,1024]{1,0:T(8,128)} slice(f32[128,1280]{1,0:T(8,128)} %shard_map.137), slice={[0:128], [0:1024]} | slice | bytes 1048576 | tf_op jit(solution)/shard_map/slice | solution.py:716
  137.4 0.6 fusion.26.head_ref
  138.0 0.9 slice.7
  139.0 0.7 copy.25
  139.7 0.0 copy-done.9
  139.7 0.6 dynamic-slice_bitcast_fusion.scale_ref
  140.3 6.5 %shard_map.138 = (f32[128,1024]{1,0:T(8,128)}, f32[49,128]{1,0:T(8,128)}, f32[1,128]{1,0:T(1,128)}, f32[150,128]{1,0:T(8,128)}) custom-call(bf16[128,1024]{1,0:T(8,128)(2,1)} %x_ref.3, f32[128,1024]{1,0:T(8,128)} %slice.6.grad_ref, f32[49,128]{1,0:T(8,128)} %bitcast.49, bf16[160,1024]{1,0:T(8,128)(2,1)} %copy-done.4, bf16[160,128]{1,0:T(8,128)(2,1)} %fusion.26.head_ref, ...), custom_call_target="tpu_custom_call" | custom-call | tf_op jit(solution)/shard_map/pallas_call | solution.py:634
  146.8 0.0 copy-done.7
  146.8 6.7 %fusion.18 = f32[512,2048]{1,0:T(8,128)} fusion(bf16[512,1024]{1,0:T(8,128)(2,1)S(1)} %copy-done.7, bf16[2048,1024]{1,0:T(8,128)(2,1)} %get-tuple-element.13.conv_ref, f32[1024]{0:T(1024)S(1)} %add_rsqrt_fusion, f32[1024]{0:T(1024)S(1)} %broadcast_multiply_fusion.2, f32[2048]{0:T(1024)S(1)} %copy-done.11), kind=kOutput, calls=%fused_computation.30 | convolution fusion | flops 2157969408 | bytes 9453568 | tf_op jit(solution)/shard_map/dot_general | solution.py:657
  153.4 2.8 %fusion.22 = f32[512,2048]{1,0:T(8,128)} fusion(bf16[512,160]{0,1:T(8,128)(2,1)S(1)} %convolution_convert_fusion.1, f32[2048]{0:T(1024)S(1)} %copy-done.9, bf16[2048,150]{0,1:T(8,128)(2,1)S(1)} %copy-done.2), kind=kOutput, calls=%fused_computation.33 | convolution fusion | flops 336527360 | bytes 4980736 | tf_op jit(solution)/shard_map/dot_general | solution.py:657
  156.2 0.6 subtract_reduce_fusion
  (4 shorter events, 0.0 us)
Async XLA Ops:
  43.0 2.9 %copy-start.11 = (f32[2048]{0:T(1024)S(1)}, f32[2048]{0:T(1024)}, u32[]{:S(2)}) copy-start(f32[2048]{0:T(1024)} %param.10) | copy-start | bytes 24580
  45.9 2.9 %copy-start = (bf16[2048,1024]{1,0:T(8,128)(2,1)S(1)}, bf16[2048,1024]{1,0:T(8,128)(2,1)}, u32[]{:S(2)}) copy-start(bf16[2048,1024]{1,0:T(8,128)(2,1)} %get-tuple-element.13.conv_ref) | copy-start | bytes 12582916
  49.5 1.6 %copy-start.6 = (bf16[512,2048]{1,0:T(8,128)(2,1)S(1)}, bf16[512,2048]{1,0:T(8,128)(2,1)}, u32[]{:S(2)}) copy-start(bf16[512,2048]{1,0:T(8,128)(2,1)} %param.12) | copy-start | bytes 6291460
  51.1 3.8 %copy-start.8 = (f32[512,160]{1,0:T(8,128)S(1)}, f32[512,160]{1,0:T(8,128)}, u32[]{:S(2)}) copy-start(f32[512,160]{1,0:T(8,128)} %get-tuple-element.14) | copy-start | bytes 983044
  54.9 1.1 copy-start.2
  54.9 1.1 copy-start.5
  55.5 26.1 %copy-start.10 = (s32[1024]{0:T(1024)S(1)}, s32[1024]{0:T(1024)}, u32[]{:S(2)}) copy-start(s32[1024]{0:T(1024)} %param.15) | copy-start | bytes 12292
  56.1 26.9 %copy-start.12 = (f32[1024,512]{0,1:T(8,128)S(1)}, f32[1024,512]{0,1:T(8,128)}, u32[]{:S(2)}) copy-start(f32[1024,512]{0,1:T(8,128)} %get-tuple-element.27) | copy-start | bytes 6291460
  83.0 5.0 %copy-start.1 = (f32[160,1024]{1,0:T(8,128)S(1)}, f32[160,1024]{1,0:T(8,128)}, u32[]{:S(2)}) copy-start(f32[160,1024]{1,0:T(8,128)} %shard_map.136) | copy-start | bytes 1966084
  87.3 1.6 %copy-start.3 = (bf16[512,2048]{1,0:T(8,128)(2,1)S(1)}, bf16[512,2048]{1,0:T(8,128)(2,1)}, u32[]{:S(2)}) copy-start(bf16[512,2048]{1,0:T(8,128)(2,1)} %w_ref.1) | copy-start | bytes 6291460
  88.2 1.2 copy-start.4
  135.4 4.3 %copy-start.9 = (f32[2048]{0:T(1024)S(1)}, f32[2048]{0:T(1024)}, u32[]{:S(2)}) copy-start(f32[2048]{0:T(1024)} %param.11) | copy-start | bytes 24580
  135.4 11.3 %copy-start.7 = (bf16[512,1024]{1,0:T(8,128)(2,1)S(1)}, bf16[512,1024]{1,0:T(8,128)(2,1)}, u32[]{:S(2)}) copy-start(bf16[512,1024]{1,0:T(8,128)(2,1)} %get-tuple-element.25.p_ref) | copy-start | bytes 3145732

commit v2 on v1

v2 whole, which is shorter than its diff:
```python
import functools
import jax
import jax.numpy as jnp
from jax import lax
from jax.experimental import pallas as pl
from jax.experimental.pallas import tpu as pltpu
from jax.sharding import PartitionSpec as P

KS = 7
WIN_H = 32
WIN_W = 32

norm_eps = 1e-06
VMEM_LIMIT = 56 * 1024 * 1024


def place(n):
    me = lax.axis_index("ch")
    return lax.div(me, 4), lax.rem(lax.div(me, 2), 2), lax.rem(me, 2)


def index_of(z, y, c):
    return (z * 2 + y) * 2 + c


LANES = 128
MOVES = WIN_H // 8
SUB = 8
PAD_W = WIN_W + 16


def fit(value, axis, length):
    short = length - value.shape[axis]
    if short == 0:
        return value
    pads = [(0, 0)] * value.ndim
    pads[axis] = (0, short)
    return jnp.pad(value, pads)


def clear_pads(grid_ref):
    half = KS // 2
    blank = jnp.zeros((half, PAD_W, LANES), jnp.float32)
    grid_ref[0:half] = blank
    grid_ref[half + WIN_H : 2 * half + WIN_H] = blank

    @pl.loop(0, WIN_H)
    def _(h):
        edge = jnp.zeros((SUB, LANES), jnp.float32)
        grid_ref[half + h, 0:SUB, :] = edge
        grid_ref[half + h, SUB + WIN_W : PAD_W, :] = edge


def put_strip(grid_ref, strip, block):
    half = KS // 2
    turned = block.T
    for r in range(LANES // WIN_W):
        grid_ref[half + strip * (LANES // WIN_W) + r, SUB : SUB + WIN_W, :] = turned[
            r * WIN_W : (r + 1) * WIN_W
        ]


def spread_taps(taps_ref, wide_ref):
    for k in range(KS * KS):
        wide_ref[k] = jnp.broadcast_to(taps_ref[k : k + 1, :], (SUB, LANES))


ROWS_AT_ONCE = 8


def conv_piece(grid_ref, taps_ref, first, col, flip=False):
    outs = [None] * ROWS_AT_ONCE
    for j in range(KS):
        start = SUB + col + j - KS // 2
        seen = [
            grid_ref[first + r, start : start + SUB, :] for r in range(ROWS_AT_ONCE + KS - 1)
        ]
        for i in range(KS):
            k = i * KS + j
            tap = taps_ref[KS * KS - 1 - k if flip else k]
            for r in range(ROWS_AT_ONCE):
                term = tap * seen[r + i]
                outs[r] = term if outs[r] is None else outs[r] + term
    return outs


def tail_kernel(
    x_ref, grad_ref, taps_ref, lg_ref, head_ref, seen_ref, scale_ref, loss_ref, dwi_ref, dwo_ref,
    dx_ref, dtaps_ref, dscale_ref, dhead_ref, mean_ref, dwi_out, dwo_out,
    x_grid, g_grid, turned, wide, taps, sums, dwi_buf, dwo_buf, move_sem
):
    rows, tokens = x_ref.shape
    tall = dwi_ref.shape[0] // MOVES
    through = ((dwi_ref, dwi_buf, dwi_out), (dwo_ref, dwo_buf, dwo_out))

    def fetch(i, k):
        own = rows_of(k, tall)
        return pltpu.make_async_copy(through[i][0].at[own], through[i][1].at[own], move_sem.at[0, i, k])

    def put(i, k):
        own = rows_of(k, tall)
        return pltpu.make_async_copy(through[i][1].at[own], through[i][2].at[own], move_sem.at[1, i, k])

    for k in range(MOVES):
        for i in range(2):
            fetch(i, k).start()
    mean_ref[...] = jnp.sum(loss_ref[...], axis=1, keepdims=True) * (1.0 / tokens)
    strips = tokens // LANES
    wide[...] = jnp.zeros_like(wide)
    wide[0:rows, :] = x_ref[...].astype(jnp.float32)
    spread_taps(taps_ref, taps)
    clear_pads(x_grid)
    clear_pads(g_grid)
    for s in range(strips):
        put_strip(x_grid, s, wide[:, s * LANES : (s + 1) * LANES])
        put_strip(g_grid, s, grad_ref[:, s * LANES : (s + 1) * LANES])
    sums[...] = jnp.zeros_like(sums)
    half = KS // 2

    @pl.loop(0, WIN_H // ROWS_AT_ONCE)
    def _(block):
        for i in range(2):
            fetch(i, block).wait()
            put(i, block).start()
        first = block * ROWS_AT_ONCE
        for col in range(0, WIN_W, SUB):
            outs = conv_piece(g_grid, taps, first, col, flip=True)
            for r in range(ROWS_AT_ONCE):
                turned[first + r, col : col + SUB, :] = outs[r]
            grads = [
                g_grid[first + half + r, SUB + col : SUB + col + SUB, :]
                for r in range(ROWS_AT_ONCE)
            ]
            for j in range(KS):
                start = SUB + col + j - half
                seen = [
                    x_grid[first + r, start : start + SUB, :]
                    for r in range(ROWS_AT_ONCE + KS - 1)
                ]
                for i in range(KS):
                    total = sums[i * KS + j]
                    for r in range(ROWS_AT_ONCE):
                        total = total + grads[r] * seen[r + i]
                    sums[i * KS + j] = total

    for k in range(KS * KS):
        dtaps_ref[k : k + 1, :] = jnp.sum(sums[k], axis=0, keepdims=True)

    head = head_ref[...].astype(jnp.float32).T.astype(jnp.bfloat16)
    per = LANES // WIN_W
    for s in range(strips):
        own = slice(s * LANES, (s + 1) * LANES)
        back = jnp.concatenate([turned[s * per + r] for r in range(per)], axis=0).T
        out_grad = jnp.dot(head, lg_ref[:, own], preferred_element_type=jnp.float32)
        dx_ref[:, own] = (back + out_grad)[0:rows]
    direct = lax.dot_general(
        lg_ref[...], wide[...].astype(jnp.bfloat16), (((1,), (1,)), ((), ())),
        preferred_element_type=jnp.float32,
    )
    seen = seen_ref[...]
    classes = dhead_ref.shape[0]
    dhead_ref[...] = (direct + scale_ref[...] * seen)[0:classes]
    dscale_ref[...] = jnp.sum(head_ref[...].astype(jnp.float32) * seen, axis=0, keepdims=True)
    for k in range(MOVES):
        for i in range(2):
            put(i, k).wait()


def tail(classes, x, grad, taps, lg, head, seen, scale, loss, d_w_in, d_w_out):
    rows, tokens = x.shape
    vmem = pl.BlockSpec(memory_space=pltpu.VMEM)
    hbm = pl.BlockSpec(memory_space=pl.ANY)
    return pl.pallas_call(
        tail_kernel,
        out_shape=(
            jax.ShapeDtypeStruct((rows, tokens), jnp.float32),
            jax.ShapeDtypeStruct((KS * KS, LANES), jnp.float32),
            jax.ShapeDtypeStruct((1, LANES), jnp.float32),
            jax.ShapeDtypeStruct((classes, LANES), jnp.float32),
            jax.ShapeDtypeStruct((1, 1), jnp.float32),
            jax.ShapeDtypeStruct(d_w_in.shape, jnp.float32),
            jax.ShapeDtypeStruct(d_w_out.shape, jnp.float32),
        ),
        in_specs=[vmem] * 8 + [hbm] * 2,
        out_specs=(vmem,) * 5 + (hbm,) * 2,
        scratch_shapes=[
            pltpu.VMEM((WIN_H + KS - 1, PAD_W, LANES), jnp.float32),
            pltpu.VMEM((WIN_H + KS - 1, PAD_W, LANES), jnp.float32),
            pltpu.VMEM((WIN_H, WIN_W, LANES), jnp.float32),
            pltpu.VMEM((LANES, tokens), jnp.float32),
            pltpu.VMEM((KS * KS, SUB, LANES), jnp.float32),
            pltpu.VMEM((KS * KS, SUB, LANES), jnp.float32),
            pltpu.VMEM(d_w_in.shape, jnp.float32),
            pltpu.VMEM(d_w_out.shape, jnp.float32),
            pltpu.SemaphoreType.DMA((2, 2, MOVES)),
        ],
        compiler_params=pltpu.CompilerParams(vmem_limit_bytes=VMEM_LIMIT),
    )(x, grad, taps, lg, head, seen, scale, loss, d_w_in, d_w_out)


PARTS = 2
SQRT_HALF = 0.7071067811865476
NORMAL = 0.3989422804014327


def lanes_of(j, size=LANES):
    return pl.ds(pl.multiple_of(j * size, size), size)


def rows_of(j, size):
    return pl.ds(pl.multiple_of(j * size, size), size)


def nt_dot(lhs, rhs):
    return lax.dot_general(lhs, rhs, (((1,), (1,)), ((), ())), preferred_element_type=jnp.float32)


def nn_dot(lhs, rhs):
    return jnp.dot(lhs, rhs, preferred_element_type=jnp.float32)


def three_parts(value):
    high = value.astype(jnp.bfloat16)
    rest = value - high.astype(jnp.float32)
    middle = rest.astype(jnp.bfloat16)
    low = (rest - middle.astype(jnp.float32)).astype(jnp.bfloat16)
    return high, middle, low


def stack_rows(parts, height, width):
    row = lax.broadcasted_iota(jnp.int32, (height, width), 0)
    out = jnp.zeros((height, width), jnp.float32)
    for i, part in enumerate(parts):
        out = jnp.where(row == i, part.astype(jnp.float32), out)
    return out.astype(jnp.bfloat16)


def block_kernel(
    n, class_count,
    x_ref, taps_ref, gain_ref, scale_ref, labels_ref, own_head_ref, head_hbm, w_in_hbm, w_out_hbm,
    land_ref, seen_ref, lg_ref, loss_ref, dwi_hbm, dwo_hbm,
    head_ref, w_in_ref, w_out_ref, load_sem,
    x_grid, wide, taps, turned,
    conv_all, wg, wg_turned, acc, gains, stats, token_rows,
    sh_high, sh_low, mix_high, mix_low, mix,
    hidden, slope, narrow, back_rows, seen_narrow,
    tw_keep, tw_out, tw_in, rs_out, slots, packs,
    msg, t_in, y_out, y_in, u_in, d_in, z_out, sums,
    dwi_buf, dwo_buf, store_sem,
    send_sem, recv_sem, tw_sem, rs_sem, lg_sem, f_sem,
    t_sem, y_sem, u_sem, d_sem, zs_sem,
):
    a, m = n // 4, n // 2
    rows, tokens = x_ref.shape
    units, channels = w_in_ref.shape
    strips = tokens // LANES
    classes = lg_ref.shape[0]
    pack = classes // 2
    z, y, c = place(n)
    me = index_of(z, y, c)
    chip = z * 2 + y
    twin, across = index_of(z, y, 1 - c), index_of(z, 1 - y, c)
    f32 = jnp.float32

    loads = [
        pltpu.make_async_copy(src, dst, load_sem.at[i])
        for i, (src, dst) in enumerate(
            ((w_in_hbm, w_in_ref), (head_hbm, head_ref), (w_out_hbm, w_out_ref))
        )
    ]
    barrier = pltpu.get_barrier_semaphore()
    pl.semaphore_signal(barrier, inc=1, device_id={"ch": twin})
    for d in range(1, m):
        pl.semaphore_signal(barrier, inc=1, device_id={"ch": lax.rem(chip + d, m) * 2 + c})
    for load in loads:
        load.start()

    span = tokens // PARTS
    half = KS // 2
    per = LANES // WIN_W
    if rows < LANES:
        wide[...] = jnp.zeros_like(wide)
    wide[0:rows, :] = x_ref[...].astype(f32)
    spread_taps(taps_ref, taps)
    clear_pads(x_grid)
    for s in range(strips):
        put_strip(x_grid, s, wide[:, s * LANES : (s + 1) * LANES])

    def convolve(h):
        blocks = WIN_H // ROWS_AT_ONCE // PARTS

        @pl.loop(h * blocks, (h + 1) * blocks)
        def _(block):
            first = block * ROWS_AT_ONCE
            for col in range(0, WIN_W, SUB):
                outs = conv_piece(x_grid, taps, first, col)
                for r in range(ROWS_AT_ONCE):
                    turned[first + r, col : col + SUB, :] = outs[r]

        for s in range(h * strips // PARTS, (h + 1) * strips // PARTS):
            back = jnp.concatenate([turned[s * per + r] for r in range(per)], axis=0).T
            conv_all[rows_of(me, rows), s * LANES : (s + 1) * LANES] = back[0:rows].astype(
                jnp.bfloat16
            )

    def copy(kind, b, device, h):
        piece = conv_all.at[rows_of(b, rows), pl.ds(h * span, span)]
        return pltpu.make_async_remote_copy(
            src_ref=piece,
            dst_ref=piece,
            send_sem=send_sem.at[kind, b * PARTS + h],
            recv_sem=recv_sem.at[b * PARTS + h],
            device_id={"ch": device},
        )

    for h in range(PARTS):
        convolve(h)
        if h == 0:
            pl.semaphore_wait(barrier, m)

        @pl.when(z < a - 1)
        def _():
            copy(0, me, me + 4, h).start()

        @pl.when(z > 0)
        def _():
            copy(1, me, me - 4, h).start()

        copy(2, me, across, h).start()
        copy(3, me, twin, h).start()

    loads[0].wait()
    pair = 2 * rows
    gains[...] = jnp.zeros_like(gains)
    ones = jnp.ones((pair, LANES), jnp.bfloat16)
    for p in range(m):
        own = slice(p * pair, (p + 1) * pair)
        gained = w_in_ref[:, own].astype(f32) * gain_ref[:, own]
        gained_narrow = gained.astype(jnp.bfloat16)
        wg[p] = gained_narrow
        wg_turned[p] = gained.T.astype(jnp.bfloat16)
        gains[...] += nn_dot(gained_narrow, ones)

    def mix_weights():
        loads[1].wait()
        loads[2].wait()
        scaled = head_ref[...].astype(f32) * scale_ref[...]
        high = scaled.astype(jnp.bfloat16)
        sh_high[...] = jnp.zeros_like(sh_high)
        sh_low[...] = jnp.zeros_like(sh_low)
        sh_high[0:class_count, :] = high
        sh_low[0:class_count, :] = (scaled - high.astype(f32)).astype(jnp.bfloat16)
        mixed = nt_dot(sh_high[...], w_out_ref[...]) + nt_dot(sh_low[...], w_out_ref[...])
        high = mixed.astype(jnp.bfloat16)
        mix_high[...] = high
        mix_low[...] = (mixed - high.astype(f32)).astype(jnp.bfloat16)
        mix[...] = nt_dot(w_out_ref[...], sh_high[...]).astype(jnp.bfloat16)

    def absorb(p, first=False):
        for h in range(PARTS):
            copy(3, p * 2 + 1 - c, twin, h).wait_recv()

        @pl.loop(0, tokens // (2 * LANES))
        def _(g):
            own = lanes_of(g, 2 * LANES)
            block = conv_all[rows_of(p, pair), own]
            product = nn_dot(wg[p], block)
            if first:
                acc[:, own] = product
            else:
                acc[:, own] += product
            block_wide = block.astype(f32)
            whole = jnp.sum(block_wide, axis=0, keepdims=True)
            off = block_wide - whole * (1.0 / pair)
            stats[p, 0:1, own] = whole
            stats[p, 1:2, own] = jnp.sum(off * off, axis=0, keepdims=True)

    def from_line(s, h):
        below, above = me - 4 * s, me + 4 * s

        @pl.when(z >= s)
        def _():
            copy(0, below, me, h).wait_recv()

            @pl.when(z < a - 1)
            def _():
                copy(0, below, me + 4, h).start()

            copy(2, below, across, h).start()
            copy(3, below, twin, h).start()

        @pl.when(z + s < a)
        def _():
            copy(1, above, me, h).wait_recv()

            @pl.when(z > 0)
            def _():
                copy(1, above, me - 4, h).start()

            copy(2, above, across, h).start()
            copy(3, above, twin, h).start()

    def from_across(s, h):
        def take(b):
            copy(2, b, across, h).wait_recv()
            copy(3, b, twin, h).start()

        if s == 0:
            take(across)
            return

        @pl.when(z >= s)
        def _():
            take(across - 4 * s)

        @pl.when(z + s < a)
        def _():
            take(across + 4 * s)

    def absorb_at(s, side):
        if s == 0:
            absorb(z * 2 + side, first=side is y)
            return

        @pl.when(z >= s)
        def _():
            absorb((z - s) * 2 + side)

        @pl.when(z + s < a)
        def _():
            absorb((z + s) * 2 + side)

    mingle = a <= 4
    for s in range(1, a):
        for h in range(PARTS):
            from_line(s, h)
            from_across(s - 1, h)
        if mingle:
            if s == 1:
                mix_weights()
            absorb_at(s - 1, y)
            if s > 1:
                absorb_at(s - 2, 1 - y)
    if not mingle:
        mix_weights()
    for h in range(PARTS):
        from_across(a - 1, h)
    if mingle:
        absorb_at(a - 1, y)
        if a > 1:
            absorb_at(a - 2, 1 - y)
        absorb_at(a - 1, 1 - y)
    else:
        acc[...] = jnp.zeros_like(acc)

        @pl.loop(0, m)
        def _(p):
            absorb(p)

    total = stats[0, 0:1, :]
    for p in range(1, m):
        total = total + stats[p, 0:1, :]
    tok_mean = total * (1.0 / channels)
    square = jnp.zeros_like(total)
    for p in range(m):
        off = stats[p, 0:1, :] * (1.0 / pair) - tok_mean
        square = square + stats[p, 1:2, :] + (pair * off) * off
    inv_std = 1.0 / jnp.sqrt(square * (1.0 / channels) + norm_eps)
    token_rows[0:1, :] = tok_mean
    token_rows[1:2, :] = inv_std

    step = m // strips
    base = lax.div(chip, step) if step > 1 else chip
    lane = lax.broadcasted_iota(jnp.int32, (pack, LANES), 1)
    left = lane < LANES // 2
    chunk = min(units, 64)

    def to_twin_strip(d):
        return pltpu.make_async_remote_copy(
            src_ref=tw_out.at[d], dst_ref=tw_in.at[d],
            send_sem=tw_sem.at[0, d], recv_sem=tw_sem.at[1, d], device_id={"ch": twin},
        )

    def to_owner(d, owner, source):
        return pltpu.make_async_remote_copy(
            src_ref=rs_out.at[d], dst_ref=slots.at[source],
            send_sem=rs_sem.at[0, d], recv_sem=rs_sem.at[1, source],
            device_id={"ch": owner * 2 + c},
        )

    def strip_at(d):
        return lax.rem(base + d + 1, strips)

    def activate(d):
        j = strip_at(d)
        own = lanes_of(j)
        mean_here, inv_here = token_rows[0:1, own], token_rows[1:2, own]

        @pl.loop(0, units // chunk)
        def _(g):
            piece = rows_of(g, chunk)
            pre = (acc[piece, own] - gains[piece, :] * mean_here) * inv_here
            cum_prob = 0.5 * (1.0 + lax.erf(pre * SQRT_HALF))
            density = jnp.exp(-0.5 * pre * pre) * NORMAL
            acc[piece, own] = pre
            hidden[piece, own] = (pre * cum_prob).astype(jnp.bfloat16)
            slope[piece, own] = (cum_prob + pre * density) * inv_here

        active = hidden[:, own]
        scores = (
            nn_dot(mix_high[...], active)
            + nn_dot(mix_low[...], active)
            + nn_dot(own_scores[...], x_strip(own))
        )
        upper, lower = scores[0:pack], scores[pack : 2 * pack]
        first = jnp.where(left, upper, pltpu.roll(lower, LANES // 2, 1))
        second = jnp.where(left, pltpu.roll(upper, LANES // 2, 1), lower)
        tw_keep[d] = jnp.where(c == 0, first, second)
        tw_out[d] = jnp.where(c == 0, second, first)
        to_twin_strip(d).start()

    def pass_on(d):
        owner = strip_at(d) * step
        to_twin_strip(d).wait_recv()
        rs_out[d] = tw_keep[d] + tw_in[d]
        if d < strips - 1:
            to_owner(d, owner, chip).start()
        elif step > 1:

            @pl.when(owner != chip)
            def _():
                to_owner(d, owner, chip).start()

    own_scores = own_head_ref

    def x_strip(own):
        return x_ref[:, own] if rows == LANES else wide[:, own].astype(jnp.bfloat16)

    for d in range(strips):
        activate(d)
        if d > 0:
            pass_on(d - 1)
    pass_on(strips - 1)

    def to_all(r):
        return pltpu.make_async_remote_copy(
            src_ref=packs.at[base, c], dst_ref=packs.at[base, c],
            send_sem=lg_sem.at[0, r], recv_sem=lg_sem.at[1, base],
            device_id={"ch": lax.rem(chip + r, m) * 2 + c},
        )

    def from_owner(j):
        return pltpu.make_async_remote_copy(
            src_ref=packs.at[j, c], dst_ref=packs.at[j, c],
            send_sem=lg_sem.at[0, 0], recv_sem=lg_sem.at[1, j],
            device_id={"ch": twin},
        )

    def forward(j, core):
        return pltpu.make_async_remote_copy(
            src_ref=packs.at[j, core], dst_ref=packs.at[j, core],
            send_sem=f_sem.at[0, j], recv_sem=f_sem.at[1, j],
            device_id={"ch": twin},
        )

    def own_strip():
        whole = rs_out[strips - 1]
        for r in range(1, m):
            source = lax.rem(chip + r, m)
            to_owner(0, 0, source).wait_recv()
            whole = whole + slots[source]
        row = lax.broadcasted_iota(jnp.int32, (pack, LANES), 0)
        kind = row + jnp.where(left, 0, pack)
        scores = jnp.where(kind < class_count, whole, -jnp.inf)
        label = jnp.broadcast_to(labels_ref[pl.ds(base, 1), :], (SUB, LANES))
        moved = pltpu.roll(label, LANES // 2, 1)
        label = jnp.where(left[0:SUB] == (c == 0), label, moved)[0:1]

        def both(value, join):
            value = jnp.broadcast_to(value, (SUB, LANES))
            return join(value, pltpu.roll(value, LANES // 2, 1))[0:1]

        row_max = both(jnp.max(scores, axis=0, keepdims=True), jnp.maximum)
        terms = jnp.exp(scores - row_max)
        exp_total = both(jnp.sum(terms, axis=0, keepdims=True), jnp.add)
        hit = kind == label
        picked = both(
            jnp.sum(jnp.where(hit, whole, 0.0), axis=0, keepdims=True), jnp.add
        )
        loss = jnp.log(exp_total) + row_max - picked
        grads = terms / exp_total - hit.astype(f32)
        packs[base, c, 0:pack] = grads.astype(jnp.bfloat16)
        packs[base, c, pack : pack + 16] = stack_rows(three_parts(loss), 16, LANES)
        for r in range(1, m):
            to_all(r).start()
        forward(base, c).start()

    if step > 1:
        pl.when(base * step == chip)(own_strip)
    else:
        own_strip()

    loss_ref[...] = jnp.zeros_like(loss_ref)

    def receive(d):
        j = strip_at(d)
        if d < strips - 1:
            from_owner(j).wait_recv()
            forward(j, c).start()
        elif step > 1:

            @pl.when(base * step != chip)
            def _():
                from_owner(j).wait_recv()
                forward(j, c).start()

    def go_back(d):
        j = strip_at(d)
        own = lanes_of(j)
        forward(j, 1 - c).wait_recv()
        first, second = packs[j, 0].astype(f32), packs[j, 1].astype(f32)
        loss = jnp.where(left[0:SUB], first[pack : pack + SUB], second[pack : pack + SUB])
        loss_ref[...] += jnp.sum(loss[0:3], axis=0, keepdims=True)
        first, second = first[0:pack], second[0:pack]
        upper = jnp.where(left, first, pltpu.roll(second, LANES // 2, 1))
        lower = jnp.where(left, pltpu.roll(first, LANES // 2, 1), second)
        grads = jnp.concatenate([upper, lower], axis=0).astype(jnp.bfloat16)
        lg_ref[:, own] = grads
        sum_gain, sum_both = jnp.zeros((1, LANES), f32), jnp.zeros((1, LANES), f32)
        for g in range(units // chunk):
            piece = slice(g * chunk, (g + 1) * chunk)
            value = nn_dot(mix[piece, :], grads) * slope[piece, own]
            narrow[piece, own] = value.astype(jnp.bfloat16)
            sum_gain = sum_gain + jnp.sum(gains[piece, :] * value, axis=0, keepdims=True)
            sum_both = sum_both + jnp.sum(acc[piece, own] * value, axis=0, keepdims=True)
        share = sum_both * (1.0 / channels) * token_rows[1:2, own]
        back_rows[0:1, own] = sum_gain * (1.0 / channels) - token_rows[0:1, own] * share
        back_rows[1:2, own] = share

    order_here = [strips - 1] + list(range(strips - 1))
    for i, d in enumerate(order_here):
        receive(d)
        if i > 0:
            go_back(order_here[i - 1])
    go_back(order_here[-1])

    body = strips * rows
    cuts = ((0, body // 2), (body // 2, body + classes))

    def dest(k):
        if k == a - 1:
            return z
        low = jnp.where(k < a - 1 - z, a - 1 - k, k - (a - 1 - z))
        high = jnp.where(k < z, k, a - 1 - (k - z))
        return jnp.where(2 * z < a, low, high)

    def cut(ref, h):
        return ref.at[pl.ds(cuts[h][0], cuts[h][1] - cuts[h][0])]

    def to_twin(zz, side, core, h):
        return pltpu.make_async_remote_copy(
            src_ref=cut(msg.at[index_of(zz, side, core)], h),
            dst_ref=cut(t_in.at[zz * 2 + side], h),
            send_sem=t_sem.at[0, zz * 2 + side, h],
            recv_sem=t_sem.at[1, zz * 2 + side, h],
            device_id={"ch": twin},
        )

    def to_across(k, zz, h):
        return pltpu.make_async_remote_copy(
            src_ref=cut(y_out.at[k], h),
            dst_ref=cut(y_in.at[zz], h),
            send_sem=y_sem.at[0, zz, h],
            recv_sem=y_sem.at[1, zz, h],
            device_id={"ch": across},
        )

    def along(k, zz, landing, sem, device, h):
        return pltpu.make_async_remote_copy(
            src_ref=cut(z_out.at[k], h),
            dst_ref=cut(landing.at[zz], h),
            send_sem=zs_sem.at[k, h],
            recv_sem=sem.at[zz, h],
            device_id={"ch": device},
        )

    def fill(zz, side, core, h):
        p = zz * 2 + side
        b = p * 2 + core
        count = strips // 2
        own = slice(h * count * LANES, (h + 1) * count * LANES)
        grad = nn_dot(wg_turned[p, rows_of(core, rows), :], narrow[:, own])
        term = grad - back_rows[0:1, own] - conv_all[rows_of(b, rows), own].astype(f32) * back_rows[1:2, own]
        term = term.astype(jnp.bfloat16)
        for s in range(count):
            first = (h * count + s) * rows
            msg[b, first : first + rows, :] = term[:, s * LANES : (s + 1) * LANES]

    def see():
        back = nt_dot(lg_ref[...], hidden[...]).astype(jnp.bfloat16)
        for p in range(m):
            block = nn_dot(back, w_out_ref[:, p * pair : (p + 1) * pair]).astype(jnp.bfloat16)
            for core in range(2):
                msg[p * 2 + core, body : body + classes, :] = fit(
                    block[:, core * rows : (core + 1) * rows], 1, LANES
                )

    slab = 32

    def cross(k, h):
        zz = dest(k)
        to_twin(zz, 1 - y, c, h).wait_recv()
        low, high = cuts[h]

        @pl.loop(low // slab, high // slab)
        def _(g):
            own = rows_of(g, slab)
            y_out[k, own] = (
                msg[index_of(zz, 1 - y, c), own].astype(f32)
                + t_in[zz * 2 + 1 - y, own].astype(f32)
            ).astype(jnp.bfloat16)

        to_across(k, zz, h).start()

    turns = [(k, h) for k in range(a) for h in range(2)]
    for i, (k, h) in enumerate(turns):
        fill(dest(k), 1 - y, 1 - c, h)
        if i == 1:
            see()
        to_twin(dest(k), 1 - y, 1 - c, h).start()
        fill(dest(k), 1 - y, c, h)
        if i > 0:
            cross(*turns[i - 1])
    for i, (k, h) in enumerate(turns):
        fill(dest(k), y, 1 - c, h)
        to_twin(dest(k), y, 1 - c, h).start()
        fill(dest(k), y, c, h)
        if i == 0:
            cross(*turns[-1])

    seen_narrow[...] = nt_dot(hidden[...], lg_ref[...]).astype(jnp.bfloat16)
    mean_rows = stack_rows(three_parts(token_rows[0:1, :]), 16, tokens)
    means = jnp.sum(nt_dot(narrow[...], mean_rows), axis=1, keepdims=True)

    swath = dwi_buf.shape[2]

    def store(buf, out, i, p):
        return pltpu.make_async_copy(
            buf.at[p % 2], out.at[:, pl.ds(p * swath, swath)], store_sem.at[i, p % 2]
        )

    def weights_piece(p):
        own = slice(p * swath, (p + 1) * swath)
        if p >= 2:
            store(dwi_buf, dwi_hbm, 0, p - 2).wait()
            store(dwo_buf, dwo_hbm, 1, p - 2).wait()
        dwi_buf[p % 2] = (nt_dot(narrow[...], conv_all[own, :]) - means) * gain_ref[:, own]
        store(dwi_buf, dwi_hbm, 0, p).start()
        dwo_buf[p % 2] = nn_dot(seen_narrow[...], sh_high[:, own])
        store(dwo_buf, dwo_hbm, 1, p).start()

    pieces = list(range(channels // swath))
    share = -(-len(pieces) // (2 * a - 1))

    def sum_up(zz, h):
        low, high = cuts[h]

        @pl.loop(low // slab, high // slab)
        def _(g):
            own = rows_of(g, slab)
            sums[own] = (
                msg[index_of(zz, y, c), own].astype(f32)
                + t_in[zz * 2 + y, own].astype(f32)
                + y_in[zz, own].astype(f32)
            )

    def add(landing, zz, h):
        low, high = cuts[h]

        @pl.loop(low // slab, high // slab)
        def _(g):
            own = rows_of(g, slab)
            sums[own] += landing[zz, own].astype(f32)

    for i, (k, h) in enumerate(turns):
        zz = dest(k)
        for p in pieces[i * share : (i + 1) * share]:
            weights_piece(p)
        to_twin(zz, y, c, h).wait_recv()
        to_across(k, zz, h).wait_recv()
        sum_up(zz, h)
        if k < a - 1:

            @pl.when((zz > z) & (z > 0))
            def _():
                along(k, zz, u_in, u_sem, me, h).wait_recv()
                add(u_in, zz, h)

            @pl.when((zz < z) & (z < a - 1))
            def _():
                along(k, zz, d_in, d_sem, me, h).wait_recv()
                add(d_in, zz, h)

            low, high = cuts[h]
            z_out[k, low:high] = sums[low:high].astype(jnp.bfloat16)

            @pl.when(zz > z)
            def _():
                along(k, zz, u_in, u_sem, me + 4, h).start()

            @pl.when(zz < z)
            def _():
                along(k, zz, d_in, d_sem, me - 4, h).start()

        else:

            @pl.when(z > 0)
            def _():
                along(0, z, u_in, u_sem, me, h).wait_recv()
                add(u_in, z, h)

            @pl.when(z < a - 1)
            def _():
                along(0, z, d_in, d_sem, me, h).wait_recv()
                add(d_in, z, h)

            for s in range(h * strips // 2, (h + 1) * strips // 2):
                land_ref[:, s * LANES : (s + 1) * LANES] = sums[s * rows : (s + 1) * rows, :]
    seen_ref[...] = sums[body : body + classes, :]

    for h in range(PARTS):
        for q in range(m):
            copy(3, q * 2 + c, twin, h).wait_send()
        for zz in range(a):
            copy(2, index_of(zz, y, c), across, h).wait_send()

            @pl.when((z < a - 1) & (zz <= z))
            def _():
                copy(0, index_of(zz, y, c), me + 4, h).wait_send()

            @pl.when((z > 0) & (zz >= z))
            def _():
                copy(1, index_of(zz, y, c), me - 4, h).wait_send()

    for d in range(strips):
        to_twin_strip(d).wait_send()
        if d < strips - 1:
            to_owner(d, 0, 0).wait_send()
        elif step > 1:

            @pl.when(base * step != chip)
            def _():
                to_owner(d, 0, 0).wait_send()

        forward(d, c).wait_send()

    def all_left():
        for r in range(1, m):
            to_all(r).wait_send()

    if step > 1:
        pl.when(base * step == chip)(all_left)
    else:
        all_left()
    for k, h in turns:
        zz = dest(k)
        to_twin(zz, 1 - y, 1 - c, h).wait_send()
        to_twin(zz, y, 1 - c, h).wait_send()
        to_across(k, zz, h).wait_send()
        if k < a - 1:
            along(k, zz, u_in, u_sem, me, h).wait_send()
    for p in pieces[-2:]:
        store(dwi_buf, dwi_hbm, 0, p).wait()
        store(dwo_buf, dwo_hbm, 1, p).wait()


def block(n, class_count, x, taps, gain, scale, labels, own_head, head, w_in, w_out):
    a, m = n // 4, n // 2
    rows, tokens = x.shape
    units, channels = w_in.shape
    strips = tokens // LANES
    classes = own_head.shape[0]
    pack = classes // 2
    length = strips * rows + classes
    pair = 2 * rows
    bf16, f32 = jnp.bfloat16, jnp.float32
    vmem = pl.BlockSpec(memory_space=pltpu.VMEM)
    hbm = pl.BlockSpec(memory_space=pl.ANY)
    dma = pltpu.SemaphoreType.DMA
    return pl.pallas_call(
        functools.partial(block_kernel, n, class_count),
        out_shape=(
            jax.ShapeDtypeStruct((rows, tokens), f32),
            jax.ShapeDtypeStruct((classes, LANES), f32),
            jax.ShapeDtypeStruct((classes, tokens), bf16),
            jax.ShapeDtypeStruct((1, LANES), f32),
            jax.ShapeDtypeStruct((units, channels), f32),
            jax.ShapeDtypeStruct((units, channels), f32),
        ),
        in_specs=[vmem] * 6 + [hbm] * 3,
        out_specs=(vmem,) * 4 + (hbm,) * 2,
        scratch_shapes=[
            pltpu.VMEM(head.shape, bf16),
            pltpu.VMEM(w_in.shape, bf16),
            pltpu.VMEM(w_out.shape, bf16),
            dma((3,)),
            pltpu.VMEM((WIN_H + KS - 1, PAD_W, LANES), f32),
            pltpu.VMEM((LANES, tokens), f32),
            pltpu.VMEM((KS * KS, SUB, LANES), f32),
            pltpu.VMEM((WIN_H, WIN_W, LANES), f32),
            pltpu.VMEM((n * rows, tokens), bf16),
            pltpu.VMEM((m, units, pair), bf16),
            pltpu.VMEM((m, pair, units), bf16),
            pltpu.VMEM((units, tokens), f32),
            pltpu.VMEM((units, LANES), f32),
            pltpu.VMEM((m, SUB, tokens), f32),
            pltpu.VMEM((SUB, tokens), f32),
            pltpu.VMEM((classes, channels), bf16),
            pltpu.VMEM((classes, channels), bf16),
            pltpu.VMEM((classes, units), bf16),
            pltpu.VMEM((classes, units), bf16),
            pltpu.VMEM((units, classes), bf16),
            pltpu.VMEM((units, tokens), bf16),
            pltpu.VMEM((units, tokens), f32),
            pltpu.VMEM((units, tokens), bf16),
            pltpu.VMEM((SUB, tokens), f32),
            pltpu.VMEM((units, classes), bf16),
            pltpu.VMEM((strips, pack, LANES), f32),
            pltpu.VMEM((strips, pack, LANES), f32),
            pltpu.VMEM((strips, pack, LANES), f32),
            pltpu.VMEM((strips, pack, LANES), f32),
            pltpu.VMEM((m, pack, LANES), f32),
            pltpu.VMEM((strips, 2, pack + 16, LANES), bf16),
            pltpu.VMEM((n, length, LANES), bf16),
            pltpu.VMEM((m, length, LANES), bf16),
            pltpu.VMEM((a, length, LANES), bf16),
            pltpu.VMEM((a, length, LANES), bf16),
            pltpu.VMEM((a, length, LANES), bf16),
            pltpu.VMEM((a, length, LANES), bf16),
            pltpu.VMEM((a, length, LANES), bf16),
            pltpu.VMEM((length, LANES), f32),
            pltpu.VMEM((2, units, 2 * LANES), f32),
            pltpu.VMEM((2, units, 2 * LANES), f32),
            dma((2, 2)),
            dma((4, n * PARTS)),
            dma((n * PARTS,)),
            dma((2, strips)),
            dma((2, m)),
            dma((2, m)),
            dma((2, strips)),
            dma((2, m, 2)),
            dma((2, a, 2)),
            dma((a, 2)),
            dma((a, 2)),
            dma((a, 2)),
        ],
        compiler_params=pltpu.CompilerParams(
            collective_id=0, has_side_effects=True, vmem_limit_bytes=VMEM_LIMIT
        ),
    )(x, taps, gain, scale, labels, own_head, head, w_in, w_out)


def per_device(n, features, dw_weight, norm_gain, layer_scale, w_in, w_out, w_head, labels):
    my_rows, tok_count = features.shape
    class_count = w_head.shape[1]
    classes = -(-class_count // 32) * 32
    head = w_head.T
    taps = fit(dw_weight.T, 1, LANES)
    row_offset = lax.axis_index("ch") * my_rows
    own_head = lax.dynamic_slice_in_dim(head, row_offset, my_rows, 1)
    own_head = fit(fit(own_head, 0, classes), 1, LANES)
    my_scale = fit(lax.dynamic_slice_in_dim(layer_scale, row_offset, my_rows, 0)[None, :], 1, LANES)
    conv_grad, seen, lg, loss, d_w_in, d_w_out = block(
        n, class_count, features, taps, norm_gain[None, :], layer_scale[None, :],
        labels.reshape(-1, LANES), own_head, head, w_in, w_out,
    )
    d_features, d_dw, d_scale, d_head, mean_loss, d_w_in, d_w_out = tail(
        class_count, features, fit(conv_grad, 0, LANES), taps, lg, own_head, seen, my_scale, loss, d_w_in, d_w_out
    )
    return (
        d_features, d_dw.T[:my_rows], d_scale[0, :my_rows], d_w_in, d_w_out, d_head.T[:my_rows],
        mean_loss[0],
    )


def solution(mesh):
    placed = (P("ch", "grp"), P("ch", None), P(), P(), P("ch", None), P("ch", None), P(), P("grp"))
    return jax.shard_map(
        functools.partial(per_device, mesh.shape["ch"]),
        mesh=mesh,
        in_specs=placed,
        out_specs=(
            P("ch", "grp"),
            P("ch", "grp"),
            P(("grp", "ch")),
            P(("grp", "ch"), None),
            P(("grp", "ch"), None),
            P("ch", "grp"),
            P("grp"),
        ),
        check_vma=False,
    )
```

time: 159 us -> 106 us (0.67)
  matrix products: 20.3 us -> 0 us
  local copies, waits for them, and re-layouts: 15 us -> 2.71 us
  Pallas kernels: 112 us -> 102 us
  other arithmetic: 9 us -> 0 us
  between operations: 2.62 us -> 0.83 us
    dot_general x8 -> x0, matrix products: 20.3 us -> none  [the longest x7 16.4 us: dot(): lax.dot_general(lhs, rhs, ((over[:1], over[1:]), ((), ())), precision=pre...]
    pallas_call x3 -> x1, Pallas kernels: 105 us -> 92.9 us  [block(): pl.pallas_call(functools.partial(block_kernel, n, class_count), out_shape...]
    unnamed x29 -> x0, local copies, waits for them, and re-layouts: 7.35 us -> none
    reduce_sum x5 -> x0, other arithmetic: 5.66 us -> none  [the longest x1 1.86 us: per_device(): gain_rows = jnp.sum(w_in.astype(jnp.float32) * norm_gain[None, :], axis=1)]
    slice x2 -> x0, local copies, waits for them, and re-layouts: 2.89 us -> none  [the longest x1 1.97 us: per_device(): conv_grad = fit(landed[:, :tok_count], 0, LANES)]
    pallas_call x1, Pallas kernels: 6.48 us -> 9.13 us  [tail(): pl.pallas_call(tail_kernel, out_shape=(jax.ShapeDtypeStruct((rows, tokens...]
    mul x1 -> x0, local copies, waits for them, and re-layouts: 1.77 us -> none  [per_device(): scaled_head = layer_scale[:, None] * head_pad.astype(jnp.float32)]
where the time goes in v2:
time: 106 us
  Pallas kernels  102 us (96%)
  local copies, waits for them, and re-layouts  2.71 us (3%)
    pallas_call x1, Pallas kernels, block(): pl.pallas_call(functools.partial(block_kernel, n, class_count), out_shape...  92.9 us
    pallas_call x1, Pallas kernels, tail(): pl.pallas_call(tail_kernel, out_shape=(jax.ShapeDtypeStruct((rows, tokens...  9.13 us

profile of v2, /device:TPU:0, one launch (start us, length us, event | category | flops | bytes accessed | tf_op | source)
XLA Modules:
  0.0 105.5 jit_solution(2634853435282499874)
XLA Ops:
  0.6 1.3 %dynamic-slice_bitcast_fusion.1.scale_ref = f32[1,128]{1,0:T(1,128)} fusion(f32[2048]{0:T(1024)} %param.11, s32[]{:T(128)S(6)} %select_n.4), kind=kLoop, calls=%fused_computation.1 | loop fusion | bytes 1028 | tf_op jit(solution)/shard_map/broadcast_in_dim | solution.py:972
  2.0 0.8 dynamic-slice_bitcast_fusion
  2.7 0.6 pad.4.own_head_ref.head_ref
  3.3 92.9 %shard_map.135 = (f32[128,1024]{1,0:T(8,128)}, f32[160,128]{1,0:T(8,128)}, bf16[160,1024]{1,0:T(8,128)(2,1)}, f32[1,128]{1,0:T(1,128)}, f32[512,2048]{1,0:T(8,128)}, /*index=5*/f32[512,2048]{1,0:T(8,128)}) custom-call(bf16[128,1024]{1,0:T(8,128)(2,1)} %x_ref.3, f32[49,128]{1,0:T(8,128)} %bitcast.14, f32[1,2048]{1,0:T(1,128)} %bitcast.16, ...), custom_call_target="tpu_custom_call" | custom-call | tf_op jit(solution)/shard_map/pallas_call | solution.py:890
  96.2 9.1 %shard_map.136 = (f32[128,1024]{1,0:T(8,128)}, f32[49,128]{1,0:T(8,128)}, f32[1,128]{1,0:T(1,128)}, f32[150,128]{1,0:T(8,128)}, f32[1,1]{1,0:T(1,128)}, /*index=5*/f32[512,2048]{1,0:T(8,128)}, f32[512,2048]{1,0:T(8,128)}) custom-call(bf16[128,1024]{1,0:T(8,128)(2,1)} %x_ref.3, f32[128,1024]{1,0:T(8,128)} %get-tuple-element.20.grad_ref, f32[49,128]{1,0:T(8,128)} %bitcast.15, ...), custom_call_target="tpu_custom_call" | custom-call | tf_op jit(solution)/shard_map/pallas_call | solution.py:173

commit v3 on v2

--- a/solution.py
+++ b/solution.py
@@ -11,7 +11,7 @@
 WIN_W = 32
 
 norm_eps = 1e-06
-VMEM_LIMIT = 56 * 1024 * 1024
+BLOCK_LIMIT = 53 * 1024 * 1024
 
 
 def place(n):
@@ -87,23 +87,19 @@
 def tail_kernel(
     x_ref, grad_ref, taps_ref, lg_ref, head_ref, seen_ref, scale_ref, loss_ref, dwi_ref, dwo_ref,
     dx_ref, dtaps_ref, dscale_ref, dhead_ref, mean_ref, dwi_out, dwo_out,
-    x_grid, g_grid, turned, wide, taps, sums, dwi_buf, dwo_buf, move_sem
+    x_grid, g_grid, turned, wide, taps, sums, move_sem
 ):
     rows, tokens = x_ref.shape
     tall = dwi_ref.shape[0] // MOVES
-    through = ((dwi_ref, dwi_buf, dwi_out), (dwo_ref, dwo_buf, dwo_out))
-
-    def fetch(i, k):
-        own = rows_of(k, tall)
-        return pltpu.make_async_copy(through[i][0].at[own], through[i][1].at[own], move_sem.at[0, i, k])
-
-    def put(i, k):
-        own = rows_of(k, tall)
-        return pltpu.make_async_copy(through[i][1].at[own], through[i][2].at[own], move_sem.at[1, i, k])
-
-    for k in range(MOVES):
-        for i in range(2):
-            fetch(i, k).start()
+    puts = [
+        pltpu.make_async_copy(
+            src.at[pl.ds(k * tall, tall)], dst.at[pl.ds(k * tall, tall)], move_sem.at[i, k]
+        )
+        for k in range(MOVES)
+        for i, (src, dst) in enumerate(((dwi_ref, dwi_out), (dwo_ref, dwo_out)))
+    ]
+    for put in puts:
+        put.start()
     mean_ref[...] = jnp.sum(loss_ref[...], axis=1, keepdims=True) * (1.0 / tokens)
     strips = tokens // LANES
     wide[...] = jnp.zeros_like(wide)
@@ -119,9 +115,6 @@
 
     @pl.loop(0, WIN_H // ROWS_AT_ONCE)
     def _(block):
-        for i in range(2):
-            fetch(i, block).wait()
-            put(i, block).start()
         first = block * ROWS_AT_ONCE
         for col in range(0, WIN_W, SUB):
             outs = conv_piece(g_grid, taps, first, col, flip=True)
@@ -161,15 +154,14 @@
     classes = dhead_ref.shape[0]
     dhead_ref[...] = (direct + scale_ref[...] * seen)[0:classes]
     dscale_ref[...] = jnp.sum(head_ref[...].astype(jnp.float32) * seen, axis=0, keepdims=True)
-    for k in range(MOVES):
-        for i in range(2):
-            put(i, k).wait()
+    for put in puts:
+        put.wait()
 
 
 def tail(classes, x, grad, taps, lg, head, seen, scale, loss, d_w_in, d_w_out):
     rows, tokens = x.shape
     vmem = pl.BlockSpec(memory_space=pltpu.VMEM)
-    hbm = pl.BlockSpec(memory_space=pl.ANY)
+    hbm = pl.BlockSpec(memory_space=pltpu.HBM)
     return pl.pallas_call(
         tail_kernel,
         out_shape=(
@@ -181,7 +173,7 @@
             jax.ShapeDtypeStruct(d_w_in.shape, jnp.float32),
             jax.ShapeDtypeStruct(d_w_out.shape, jnp.float32),
         ),
-        in_specs=[vmem] * 8 + [hbm] * 2,
+        in_specs=[vmem] * 10,
         out_specs=(vmem,) * 5 + (hbm,) * 2,
         scratch_shapes=[
             pltpu.VMEM((WIN_H + KS - 1, PAD_W, LANES), jnp.float32),
@@ -190,11 +182,9 @@
             pltpu.VMEM((LANES, tokens), jnp.float32),
             pltpu.VMEM((KS * KS, SUB, LANES), jnp.float32),
             pltpu.VMEM((KS * KS, SUB, LANES), jnp.float32),
-            pltpu.VMEM(d_w_in.shape, jnp.float32),
-            pltpu.VMEM(d_w_out.shape, jnp.float32),
-            pltpu.SemaphoreType.DMA((2, 2, MOVES)),
+            pltpu.SemaphoreType.DMA((2, MOVES)),
         ],
-        compiler_params=pltpu.CompilerParams(vmem_limit_bytes=VMEM_LIMIT),
+        compiler_params=pltpu.CompilerParams(vmem_limit_bytes=32 * 1024 * 1024),
     )(x, grad, taps, lg, head, seen, scale, loss, d_w_in, d_w_out)
 
 
@@ -237,16 +227,15 @@
 
 def block_kernel(
     n, class_count,
-    x_ref, taps_ref, gain_ref, scale_ref, labels_ref, own_head_ref, head_hbm, w_in_hbm, w_out_hbm,
-    land_ref, seen_ref, lg_ref, loss_ref, dwi_hbm, dwo_hbm,
-    head_ref, w_in_ref, w_out_ref, load_sem,
+    x_hbm, taps_hbm, gain_hbm, scale_hbm, labels_hbm, head_hbm, w_in_hbm, w_out_hbm,
+    land_ref, seen_ref, lg_ref, loss_ref, own_head_ref, own_scale_ref, dwi_ref, dwo_ref,
+    x_ref, taps_ref, gain_ref, scale_ref, labels_ref, head_ref, w_in_ref, w_out_ref, load_sem,
     x_grid, wide, taps, turned,
     conv_all, wg, wg_turned, acc, gains, stats, token_rows,
     sh_high, sh_low, mix_high, mix_low, mix,
     hidden, slope, narrow, back_rows, seen_narrow,
     tw_keep, tw_out, tw_in, rs_out, slots, packs,
     msg, t_in, y_out, y_in, u_in, d_in, z_out, sums,
-    dwi_buf, dwo_buf, store_sem,
     send_sem, recv_sem, tw_sem, rs_sem, lg_sem, f_sem,
     t_sem, y_sem, u_sem, d_sem, zs_sem,
 ):
@@ -265,24 +254,30 @@
     loads = [
         pltpu.make_async_copy(src, dst, load_sem.at[i])
         for i, (src, dst) in enumerate(
-            ((w_in_hbm, w_in_ref), (head_hbm, head_ref), (w_out_hbm, w_out_ref))
+            (
+                (x_hbm, x_ref), (taps_hbm, taps_ref), (w_in_hbm, w_in_ref), (gain_hbm, gain_ref),
+                (head_hbm, head_ref), (w_out_hbm, w_out_ref), (scale_hbm, scale_ref),
+                (labels_hbm, labels_ref),
+            )
         )
     ]
+    for load in loads:
+        load.start()
     barrier = pltpu.get_barrier_semaphore()
     pl.semaphore_signal(barrier, inc=1, device_id={"ch": twin})
     for d in range(1, m):
         pl.semaphore_signal(barrier, inc=1, device_id={"ch": lax.rem(chip + d, m) * 2 + c})
-    for load in loads:
-        load.start()
 
     span = tokens // PARTS
     half = KS // 2
     per = LANES // WIN_W
     if rows < LANES:
         wide[...] = jnp.zeros_like(wide)
+    clear_pads(x_grid)
+    loads[0].wait()
+    loads[1].wait()
     wide[0:rows, :] = x_ref[...].astype(f32)
     spread_taps(taps_ref, taps)
-    clear_pads(x_grid)
     for s in range(strips):
         put_strip(x_grid, s, wide[:, s * LANES : (s + 1) * LANES])
 
@@ -329,7 +324,8 @@
         copy(2, me, across, h).start()
         copy(3, me, twin, h).start()
 
-    loads[0].wait()
+    loads[2].wait()
+    loads[3].wait()
     pair = 2 * rows
     gains[...] = jnp.zeros_like(gains)
     ones = jnp.ones((pair, LANES), jnp.bfloat16)
@@ -342,8 +338,8 @@
         gains[...] += nn_dot(gained_narrow, ones)
 
     def mix_weights():
-        loads[1].wait()
-        loads[2].wait()
+        for load in loads[4:]:
+            load.wait()
         scaled = head_ref[...].astype(f32) * scale_ref[...]
         high = scaled.astype(jnp.bfloat16)
         sh_high[...] = jnp.zeros_like(sh_high)
@@ -355,6 +351,13 @@
         mix_high[...] = high
         mix_low[...] = (mixed - high.astype(f32)).astype(jnp.bfloat16)
         mix[...] = nt_dot(w_out_ref[...], sh_high[...]).astype(jnp.bfloat16)
+        channel = lax.broadcasted_iota(jnp.int32, (channels, LANES), 0) - me * rows
+        at = lax.broadcasted_iota(jnp.int32, (channels, LANES), 1)
+        chosen = ((channel == at) & (at < rows)).astype(f32).astype(jnp.bfloat16)
+        own_head_ref[...] = jnp.zeros_like(own_head_ref)
+        own_head_ref[0:class_count, :] = nn_dot(head_ref[...], chosen).astype(jnp.bfloat16)
+        scale_rows = stack_rows(three_parts(scale_ref[...]), 16, channels)
+        own_scale_ref[...] = jnp.sum(nn_dot(scale_rows, chosen), axis=0, keepdims=True)
 
     def absorb(p, first=False):
         for h in range(PARTS):
@@ -742,22 +745,12 @@
     mean_rows = stack_rows(three_parts(token_rows[0:1, :]), 16, tokens)
     means = jnp.sum(nt_dot(narrow[...], mean_rows), axis=1, keepdims=True)
 
-    swath = dwi_buf.shape[2]
-
-    def store(buf, out, i, p):
-        return pltpu.make_async_copy(
-            buf.at[p % 2], out.at[:, pl.ds(p * swath, swath)], store_sem.at[i, p % 2]
-        )
+    swath = 2 * LANES
 
     def weights_piece(p):
         own = slice(p * swath, (p + 1) * swath)
-        if p >= 2:
-            store(dwi_buf, dwi_hbm, 0, p - 2).wait()
-            store(dwo_buf, dwo_hbm, 1, p - 2).wait()
-        dwi_buf[p % 2] = (nt_dot(narrow[...], conv_all[own, :]) - means) * gain_ref[:, own]
-        store(dwi_buf, dwi_hbm, 0, p).start()
-        dwo_buf[p % 2] = nn_dot(seen_narrow[...], sh_high[:, own])
-        store(dwo_buf, dwo_hbm, 1, p).start()
+        dwi_ref[:, own] = (nt_dot(narrow[...], conv_all[own, :]) - means) * gain_ref[:, own]
+        dwo_ref[:, own] = nn_dot(seen_narrow[...], sh_high[:, own])
 
     pieces = list(range(channels // swath))
     share = -(-len(pieces) // (2 * a - 1))
@@ -869,110 +862,108 @@
         to_across(k, zz, h).wait_send()
         if k < a - 1:
             along(k, zz, u_in, u_sem, me, h).wait_send()
-    for p in pieces[-2:]:
-        store(dwi_buf, dwi_hbm, 0, p).wait()
-        store(dwo_buf, dwo_hbm, 1, p).wait()
-
-
-def block(n, class_count, x, taps, gain, scale, labels, own_head, head, w_in, w_out):
+
+
+def block(n, class_count, x, taps, gain, scale, labels, head, w_in, w_out):
     a, m = n // 4, n // 2
     rows, tokens = x.shape
     units, channels = w_in.shape
     strips = tokens // LANES
-    classes = own_head.shape[0]
+    classes = -(-class_count // 32) * 32
     pack = classes // 2
     length = strips * rows + classes
     pair = 2 * rows
     bf16, f32 = jnp.bfloat16, jnp.float32
     vmem = pl.BlockSpec(memory_space=pltpu.VMEM)
-    hbm = pl.BlockSpec(memory_space=pl.ANY)
+    hbm = pl.BlockSpec(memory_space=pltpu.HBM)
     dma = pltpu.SemaphoreType.DMA
+    scratch = [
+        pltpu.VMEM(x.shape, x.dtype),
+        pltpu.VMEM(taps.shape, taps.dtype),
+        pltpu.VMEM(gain.shape, gain.dtype),
+        pltpu.VMEM(scale.shape, scale.dtype),
+        pltpu.VMEM(labels.shape, labels.dtype),
+        pltpu.VMEM(head.shape, head.dtype),
+        pltpu.VMEM(w_in.shape, w_in.dtype),
+        pltpu.VMEM(w_out.shape, w_out.dtype),
+        dma((8,)),
+        pltpu.VMEM((WIN_H + KS - 1, PAD_W, LANES), f32),
+        pltpu.VMEM((LANES, tokens), f32),
+        pltpu.VMEM((KS * KS, SUB, LANES), f32),
+        pltpu.VMEM((WIN_H, WIN_W, LANES), f32),
+        pltpu.VMEM((n * rows, tokens), bf16),
+        pltpu.VMEM((m, units, pair), bf16),
+        pltpu.VMEM((m, pair, units), bf16),
+        pltpu.VMEM((units, tokens), f32),
+        pltpu.VMEM((units, LANES), f32),
+        pltpu.VMEM((m, SUB, tokens), f32),
+        pltpu.VMEM((SUB, tokens), f32),
+        pltpu.VMEM((classes, channels), bf16),
+        pltpu.VMEM((classes, channels), bf16),
+        pltpu.VMEM((classes, units), bf16),
+        pltpu.VMEM((classes, units), bf16),
+        pltpu.VMEM((units, classes), bf16),
+        pltpu.VMEM((units, tokens), bf16),
+        pltpu.VMEM((units, tokens), f32),
+        pltpu.VMEM((units, tokens), bf16),
+        pltpu.VMEM((SUB, tokens), f32),
+        pltpu.VMEM((units, classes), bf16),
+        pltpu.VMEM((strips, pack, LANES), f32),
+        pltpu.VMEM((strips, pack, LANES), f32),
+        pltpu.VMEM((strips, pack, LANES), f32),
+        pltpu.VMEM((strips, pack, LANES), f32),
+        pltpu.VMEM((m, pack, LANES), f32),
+        pltpu.VMEM((strips, 2, pack + 16, LANES), bf16),
+        pltpu.VMEM((n, length, LANES), bf16),
+        pltpu.VMEM((m, length, LANES), bf16),
+        pltpu.VMEM((a, length, LANES), bf16),
+        pltpu.VMEM((a, length, LANES), bf16),
+        pltpu.VMEM((a, length, LANES), bf16),
+        pltpu.VMEM((a, length, LANES), bf16),
+        pltpu.VMEM((a, length, LANES), bf16),
+        pltpu.VMEM((length, LANES), f32),
+        dma((4, n * PARTS)),
+        dma((n * PARTS,)),
+        dma((2, strips)),
+        dma((2, m)),
+        dma((2, m)),
+        dma((2, strips)),
+        dma((2, m, 2)),
+        dma((2, a, 2)),
+        dma((a, 2)),
+        dma((a, 2)),
+        dma((a, 2)),
+    ]
     return pl.pallas_call(
         functools.partial(block_kernel, n, class_count),
         out_shape=(
-            jax.ShapeDtypeStruct((rows, tokens), f32),
-            jax.ShapeDtypeStruct((classes, LANES), f32),
-            jax.ShapeDtypeStruct((classes, tokens), bf16),
-            jax.ShapeDtypeStruct((1, LANES), f32),
-            jax.ShapeDtypeStruct((units, channels), f32),
-            jax.ShapeDtypeStruct((units, channels), f32),
+            pltpu.VMEM((rows, tokens), f32),
+            pltpu.VMEM((classes, LANES), f32),
+            pltpu.VMEM((classes, tokens), bf16),
+            pltpu.VMEM((1, LANES), f32),
+            pltpu.VMEM((classes, LANES), bf16),
+            pltpu.VMEM((1, LANES), f32),
+            pltpu.VMEM((units, channels), f32),
+            pltpu.VMEM((units, channels), f32),
         ),
-        in_specs=[vmem] * 6 + [hbm] * 3,
-        out_specs=(vmem,) * 4 + (hbm,) * 2,
-        scratch_shapes=[
-            pltpu.VMEM(head.shape, bf16),
-            pltpu.VMEM(w_in.shape, bf16),
-            pltpu.VMEM(w_out.shape, bf16),
-            dma((3,)),
-            pltpu.VMEM((WIN_H + KS - 1, PAD_W, LANES), f32),
-            pltpu.VMEM((LANES, tokens), f32),
-            pltpu.VMEM((KS * KS, SUB, LANES), f32),
-            pltpu.VMEM((WIN_H, WIN_W, LANES), f32),
-            pltpu.VMEM((n * rows, tokens), bf16),
-            pltpu.VMEM((m, units, pair), bf16),
-            pltpu.VMEM((m, pair, units), bf16),
-            pltpu.VMEM((units, tokens), f32),
-            pltpu.VMEM((units, LANES), f32),
-            pltpu.VMEM((m, SUB, tokens), f32),
-            pltpu.VMEM((SUB, tokens), f32),
-            pltpu.VMEM((classes, channels), bf16),
-            pltpu.VMEM((classes, channels), bf16),
-            pltpu.VMEM((classes, units), bf16),
-            pltpu.VMEM((classes, units), bf16),
-            pltpu.VMEM((units, classes), bf16),
-            pltpu.VMEM((units, tokens), bf16),
-            pltpu.VMEM((units, tokens), f32),
-            pltpu.VMEM((units, tokens), bf16),
-            pltpu.VMEM((SUB, tokens), f32),
-            pltpu.VMEM((units, classes), bf16),
-            pltpu.VMEM((strips, pack, LANES), f32),
-            pltpu.VMEM((strips, pack, LANES), f32),
-            pltpu.VMEM((strips, pack, LANES), f32),
-            pltpu.VMEM((strips, pack, LANES), f32),
-            pltpu.VMEM((m, pack, LANES), f32),
-            pltpu.VMEM((strips, 2, pack + 16, LANES), bf16),
-            pltpu.VMEM((n, length, LANES), bf16),
-            pltpu.VMEM((m, length, LANES), bf16),
-            pltpu.VMEM((a, length, LANES), bf16),
-            pltpu.VMEM((a, length, LANES), bf16),
-            pltpu.VMEM((a, length, LANES), bf16),
-            pltpu.VMEM((a, length, LANES), bf16),
-            pltpu.VMEM((a, length, LANES), bf16),
-            pltpu.VMEM((length, LANES), f32),
-            pltpu.VMEM((2, units, 2 * LANES), f32),
-            pltpu.VMEM((2, units, 2 * LANES), f32),
-            dma((2, 2)),
-            dma((4, n * PARTS)),
-            dma((n * PARTS,)),
-            dma((2, strips)),
-            dma((2, m)),
-            dma((2, m)),
-            dma((2, strips)),
-            dma((2, m, 2)),
-            dma((2, a, 2)),
-            dma((a, 2)),
-            dma((a, 2)),
-            dma((a, 2)),
-        ],
+        in_specs=[hbm] * 8,
+        out_specs=(vmem,) * 8,
+        scratch_shapes=scratch,
         compiler_params=pltpu.CompilerParams(
-            collective_id=0, has_side_effects=True, vmem_limit_bytes=VMEM_LIMIT
+            collective_id=0, has_side_effects=True,
+            vmem_limit_bytes=BLOCK_LIMIT,
         ),
-    )(x, taps, gain, scale, labels, own_head, head, w_in, w_out)
+    )(x, taps, gain, scale, labels, head, w_in, w_out)
 
 
 def per_device(n, features, dw_weight, norm_gain, layer_scale, w_in, w_out, w_head, labels):
     my_rows, tok_count = features.shape
     class_count = w_head.shape[1]
-    classes = -(-class_count // 32) * 32
     head = w_head.T
     taps = fit(dw_weight.T, 1, LANES)
-    row_offset = lax.axis_index("ch") * my_rows
-    own_head = lax.dynamic_slice_in_dim(head, row_offset, my_rows, 1)
-    own_head = fit(fit(own_head, 0, classes), 1, LANES)
-    my_scale = fit(lax.dynamic_slice_in_dim(layer_scale, row_offset, my_rows, 0)[None, :], 1, LANES)
-    conv_grad, seen, lg, loss, d_w_in, d_w_out = block(
+    conv_grad, seen, lg, loss, own_head, my_scale, d_w_in, d_w_out = block(
         n, class_count, features, taps, norm_gain[None, :], layer_scale[None, :],
-        labels.reshape(-1, LANES), own_head, head, w_in, w_out,
+        labels.reshape(-1, LANES), head, w_in, w_out,
     )
     d_features, d_dw, d_scale, d_head, mean_loss, d_w_in, d_w_out = tail(
         class_count, features, fit(conv_grad, 0, LANES), taps, lg, own_head, seen, my_scale, loss, d_w_in, d_w_out

time: 106 us -> 97.5 us (0.920)
  Pallas kernels: 102 us -> 96.5 us
  local copies, waits for them, and re-layouts: 2.71 us -> 0.01 us
    pallas_call x1, Pallas kernels: 9.13 us -> 5.44 us  [tail(): pl.pallas_call(tail_kernel, out_shape=(jax.ShapeDtypeStruct((rows, tokens...]
    pallas_call x1, Pallas kernels: 92.9 us -> 91.1 us  [block(): pl.pallas_call(functools.partial(block_kernel, n, class_count), out_shape...]
    broadcast_in_dim x1 -> x0, local copies, waits for them, and re-layouts: 1.32 us -> none  [per_device(): lax.dynamic_slice_in_dim(layer_scale, row_offset, my_rows, 0)[None, :]]
where the time goes in v3:
time: 97.5 us; the launch traced here: 97.4 us
  Pallas kernels  96.5 us (99%)
    pallas_call x1, Pallas kernels, block(): pl.pallas_call(functools.partial(block_kernel, n, class_count), out_shape...  91.1 us
    pallas_call x1, Pallas kernels, tail(): pl.pallas_call(tail_kernel, out_shape=(jax.ShapeDtypeStruct((rows, tokens...  5.44 us

profile of v3, /device:TPU:0, one launch (start us, length us, event | category | flops | bytes accessed | tf_op | source)
XLA Modules:
  0.0 97.4 jit_solution(8785222440137543450)
XLA Ops:
  0.6 0.0 copy-start
  0.6 0.0 copy-start.1
  0.7 91.1 %shard_map.135 = (f32[128,1024]{1,0:T(8,128)S(1)}, f32[160,128]{1,0:T(8,128)S(1)}, bf16[160,1024]{1,0:T(8,128)(2,1)S(1)}, f32[1,128]{1,0:T(1,128)S(1)}, bf16[160...) custom-call(bf16[128,1024]{1,0:T(8,128)(2,1)} %x_ref.1, ...), custom_call_target="tpu_custom_call" | custom-call | tf_op jit(solution)/shard_map/pallas_call | solution.py:937
  91.8 0.0 copy-done
  91.8 0.0 copy-done.1
  91.8 5.4 %shard_map.136 = (f32[128,1024]{1,0:T(8,128)}, f32[49,128]{1,0:T(8,128)}, f32[1,128]{1,0:T(1,128)}, f32[150,128]{1,0:T(8,128)}, f32[1,1]{1,0:T(1,128)}, /*index=5*/f32[512,2048]{1,0:T(8,128)}, f32[512,2048]{1,0:T(8,128)}) custom-call(bf16[128,1024]{1,0:T(8,128)(2,1)S(1)} %copy-done, f32[128,1024]{1,0:T(8,128)S(1)} %get-tuple-element.22.grad_ref, ...), custom_call_target="tpu_custom_call" | custom-call | tf_op jit(solution)/shard_map/pallas_call | solution.py:165
Async XLA Ops:
  0.6 91.1 %copy-start = (bf16[128,1024]{1,0:T(8,128)(2,1)S(1)}, bf16[128,1024]{1,0:T(8,128)(2,1)}, u32[]{:S(2)}) copy-start(bf16[128,1024]{1,0:T(8,128)(2,1)} %x_ref.1) | copy-start | bytes 786436
  0.6 91.1 %copy-start.1 = (f32[128,49]{0,1:T(8,128)S(1)}, f32[128,49]{0,1:T(8,128)}, u32[]{:S(2)}) copy-start(f32[128,49]{0,1:T(8,128)} %param.9) | copy-start | bytes 75268

commit v4 on v3

--- a/solution.py
+++ b/solution.py
@@ -237,7 +237,7 @@
     tw_keep, tw_out, tw_in, rs_out, slots, packs,
     msg, t_in, y_out, y_in, u_in, d_in, z_out, sums,
     send_sem, recv_sem, tw_sem, rs_sem, lg_sem, f_sem,
-    t_sem, y_sem, u_sem, d_sem, zs_sem,
+    t_sem, y_sem, u_sem, d_sem, zs_sem, m_in, m_sem,
 ):
     a, m = n // 4, n // 2
     rows, tokens = x_ref.shape
@@ -308,6 +308,33 @@
             device_id={"ch": device},
         )
 
+    balance = a == 4
+    odd = lax.rem(z, 2) == 1
+    mate = jnp.where(odd, z - 1, z + 1)
+    end = (z == 0) | (z == a - 1)
+
+    def to_mate(h):
+        return copy(4, across, index_of(mate, y, c), h)
+
+    def when_by_line(own_end, h, then):
+        if 2 * h >= PARTS:
+            then()
+        else:
+            pl.when(jnp.logical_not(own_end))(then)
+
+    def send_across(b, below, s, h):
+        def go():
+            copy(2, b, across, h).start()
+
+        if not balance or s > 1:
+            go()
+            return
+        is_mate = odd if below else jnp.logical_not(odd)
+        if 2 * h >= PARTS:
+            pl.when(jnp.logical_not(is_mate))(go)
+        else:
+            pl.when(jnp.logical_not(is_mate) | end)(go)
+
     for h in range(PARTS):
         convolve(h)
         if h == 0:
@@ -337,7 +364,7 @@
         wg_turned[p] = gained.T.astype(jnp.bfloat16)
         gains[...] += nn_dot(gained_narrow, ones)
 
-    def mix_weights():
+    def scale_head():
         for load in loads[4:]:
             load.wait()
         scaled = head_ref[...].astype(f32) * scale_ref[...]
@@ -346,10 +373,14 @@
         sh_low[...] = jnp.zeros_like(sh_low)
         sh_high[0:class_count, :] = high
         sh_low[0:class_count, :] = (scaled - high.astype(f32)).astype(jnp.bfloat16)
+
+    def mix_head():
         mixed = nt_dot(sh_high[...], w_out_ref[...]) + nt_dot(sh_low[...], w_out_ref[...])
         high = mixed.astype(jnp.bfloat16)
         mix_high[...] = high
         mix_low[...] = (mixed - high.astype(f32)).astype(jnp.bfloat16)
+
+    def mix_back():
         mix[...] = nt_dot(w_out_ref[...], sh_high[...]).astype(jnp.bfloat16)
         channel = lax.broadcasted_iota(jnp.int32, (channels, LANES), 0) - me * rows
         at = lax.broadcasted_iota(jnp.int32, (channels, LANES), 1)
@@ -389,7 +420,7 @@
             def _():
                 copy(0, below, me + 4, h).start()
 
-            copy(2, below, across, h).start()
+            send_across(below, True, s, h)
             copy(3, below, twin, h).start()
 
         @pl.when(z + s < a)
@@ -400,7 +431,7 @@
             def _():
                 copy(1, above, me - 4, h).start()
 
-            copy(2, above, across, h).start()
+            send_across(above, False, s, h)
             copy(3, above, twin, h).start()
 
     def from_across(s, h):
@@ -410,6 +441,16 @@
 
         if s == 0:
             take(across)
+            if balance:
+                pl.when(end)(lambda: to_mate(h).start())
+            return
+
+        if balance and s == 1 and 2 * h >= PARTS:
+            @pl.when(jnp.logical_not(end))
+            def _():
+                take(across - 4)
+                take(across + 4)
+
             return
 
         @pl.when(z >= s)
@@ -433,27 +474,48 @@
         def _():
             absorb((z + s) * 2 + side)
 
-    mingle = a <= 4
+    def absorb_beside(inner):
+        @pl.when(jnp.logical_not(end) if inner else end)
+        def _():
+            absorb(mate * 2 + 1 - y)
+            if inner:
+                absorb((2 * z - mate) * 2 + 1 - y)
+
+    work = {
+        (1, 0): [scale_head],
+        (1, 1): [mix_head],
+        (2, 0): [mix_back],
+        (2, 1): [lambda: absorb_at(0, y), lambda: absorb_at(0, 1 - y)],
+        (3, 0): [lambda: absorb_at(1, y)],
+        (3, 1): [lambda: absorb_at(2, y), lambda: absorb_beside(True)],
+    }
     for s in range(1, a):
         for h in range(PARTS):
             from_line(s, h)
             from_across(s - 1, h)
-        if mingle:
-            if s == 1:
-                mix_weights()
-            absorb_at(s - 1, y)
-            if s > 1:
-                absorb_at(s - 2, 1 - y)
-    if not mingle:
-        mix_weights()
+            if balance and s == a - 2 and 2 * h >= PARTS:
+                pl.when(jnp.logical_not(end))(lambda: to_mate(h).start())
+            for item in work.get((s, h), []) if balance else []:
+                item()
     for h in range(PARTS):
         from_across(a - 1, h)
-    if mingle:
-        absorb_at(a - 1, y)
-        if a > 1:
-            absorb_at(a - 2, 1 - y)
-        absorb_at(a - 1, 1 - y)
+    if balance:
+
+        @pl.when(end)
+        def _():
+            for h in range(PARTS // 2, PARTS):
+                block_there = index_of(mate, 1 - y, c)
+                copy(2, block_there, across, h).wait_recv()
+                copy(3, block_there, twin, h).start()
+
+        absorb_at(2, 1 - y)
+        absorb_at(3, y)
+        absorb_at(3, 1 - y)
+        absorb_beside(False)
     else:
+        scale_head()
+        mix_head()
+        mix_back()
         acc[...] = jnp.zeros_like(acc)
 
         @pl.loop(0, m)
@@ -710,6 +772,15 @@
 
     slab = 32
 
+    def sums_to_mate(h):
+        return pltpu.make_async_remote_copy(
+            src_ref=cut(y_out.at[a - 2], h),
+            dst_ref=cut(m_in, h),
+            send_sem=m_sem.at[0, h],
+            recv_sem=m_sem.at[1, h],
+            device_id={"ch": index_of(mate, y, c)},
+        )
+
     def cross(k, h):
         zz = dest(k)
         to_twin(zz, 1 - y, c, h).wait_recv()
@@ -723,23 +794,52 @@
                 + t_in[zz * 2 + 1 - y, own].astype(f32)
             ).astype(jnp.bfloat16)
 
+        if not balance:
+            to_across(k, zz, h).start()
+            return
+        if k == a - 2:
+            when_by_line(end, h, lambda: sums_to_mate(h).start())
+            if h == 0:
+                pl.when(end)(lambda: to_across(k, zz, h).start())
+            return
+        if k == a - 1:
+
+            def join():
+                sums_to_mate(h).wait_recv()
+
+                @pl.loop(low // slab, high // slab)
+                def _(g):
+                    own = rows_of(g, slab)
+                    y_out[k, own] = (y_out[k, own].astype(f32) + m_in[own].astype(f32)).astype(
+                        jnp.bfloat16
+                    )
+
+            when_by_line(jnp.logical_not(end), h, join)
         to_across(k, zz, h).start()
 
     turns = [(k, h) for k in range(a) for h in range(2)]
-    for i, (k, h) in enumerate(turns):
+    if balance:
+        crossings = [(0, 0), (2, 1), (0, 1), (2, 0), (1, 0), (1, 1), (3, 0), (3, 1)]
+        late = crossings[-2:]
+    else:
+        crossings, late = turns, []
+    ready = []
+    for i, (k, h) in enumerate(crossings):
         fill(dest(k), 1 - y, 1 - c, h)
         if i == 1:
             see()
         to_twin(dest(k), 1 - y, 1 - c, h).start()
         fill(dest(k), 1 - y, c, h)
-        if i > 0:
-            cross(*turns[i - 1])
+        if ready:
+            cross(*ready.pop())
+        if (k, h) not in late:
+            ready.append((k, h))
     for i, (k, h) in enumerate(turns):
         fill(dest(k), y, 1 - c, h)
         to_twin(dest(k), y, 1 - c, h).start()
         fill(dest(k), y, c, h)
-        if i == 0:
-            cross(*turns[-1])
+        if ready:
+            cross(*ready.pop())
 
     seen_narrow[...] = nt_dot(hidden[...], lg_ref[...]).astype(jnp.bfloat16)
     mean_rows = stack_rows(three_parts(token_rows[0:1, :]), 16, tokens)
@@ -755,17 +855,14 @@
     pieces = list(range(channels // swath))
     share = -(-len(pieces) // (2 * a - 1))
 
-    def sum_up(zz, h):
+    def sum_up(zz, h, with_across):
         low, high = cuts[h]
 
         @pl.loop(low // slab, high // slab)
         def _(g):
             own = rows_of(g, slab)
-            sums[own] = (
-                msg[index_of(zz, y, c), own].astype(f32)
-                + t_in[zz * 2 + y, own].astype(f32)
-                + y_in[zz, own].astype(f32)
-            )
+            total = msg[index_of(zz, y, c), own].astype(f32) + t_in[zz * 2 + y, own].astype(f32)
+            sums[own] = total + y_in[zz, own].astype(f32) if with_across else total
 
     def add(landing, zz, h):
         low, high = cuts[h]
@@ -780,8 +877,17 @@
         for p in pieces[i * share : (i + 1) * share]:
             weights_piece(p)
         to_twin(zz, y, c, h).wait_recv()
-        to_across(k, zz, h).wait_recv()
-        sum_up(zz, h)
+        with_across = not (balance and k == a - 2)
+        if with_across:
+            to_across(k, zz, h).wait_recv()
+        sum_up(zz, h, with_across)
+        if not with_across and h == 0:
+
+            @pl.when(end)
+            def _():
+                to_across(k, zz, h).wait_recv()
+                add(y_in, zz, h)
+
         if k < a - 1:
 
             @pl.when((zz > z) & (z > 0))
@@ -819,13 +925,26 @@
 
             for s in range(h * strips // 2, (h + 1) * strips // 2):
                 land_ref[:, s * LANES : (s + 1) * LANES] = sums[s * rows : (s + 1) * rows, :]
+        if i == 1:
+            for crossing in late:
+                cross(*crossing)
     seen_ref[...] = sums[body : body + classes, :]
 
     for h in range(PARTS):
         for q in range(m):
             copy(3, q * 2 + c, twin, h).wait_send()
+        if balance:
+            when_by_line(jnp.logical_not(end), h, lambda: to_mate(h).wait_send())
         for zz in range(a):
-            copy(2, index_of(zz, y, c), across, h).wait_send()
+            if balance:
+                crossed = (zz != mate) if 2 * h >= PARTS else ((zz != mate) | end)
+
+                @pl.when(crossed)
+                def _():
+                    copy(2, index_of(zz, y, c), across, h).wait_send()
+
+            else:
+                copy(2, index_of(zz, y, c), across, h).wait_send()
 
             @pl.when((z < a - 1) & (zz <= z))
             def _():
@@ -859,7 +978,12 @@
         zz = dest(k)
         to_twin(zz, 1 - y, 1 - c, h).wait_send()
         to_twin(zz, y, 1 - c, h).wait_send()
-        to_across(k, zz, h).wait_send()
+        if balance and k == a - 2:
+            when_by_line(end, h, lambda: sums_to_mate(h).wait_send())
+            if h == 0:
+                pl.when(end)(lambda: to_across(k, zz, h).wait_send())
+        else:
+            to_across(k, zz, h).wait_send()
         if k < a - 1:
             along(k, zz, u_in, u_sem, me, h).wait_send()
 
@@ -922,7 +1046,7 @@
         pltpu.VMEM((a, length, LANES), bf16),
         pltpu.VMEM((a, length, LANES), bf16),
         pltpu.VMEM((length, LANES), f32),
-        dma((4, n * PARTS)),
+        dma((5, n * PARTS)),
         dma((n * PARTS,)),
         dma((2, strips)),
         dma((2, m)),
@@ -933,6 +1057,8 @@
         dma((a, 2)),
         dma((a, 2)),
         dma((a, 2)),
+        pltpu.VMEM((length, LANES), bf16),
+        dma((2, 2)),
     ]
     return pl.pallas_call(
         functools.partial(block_kernel, n, class_count),

time: 97.5 us -> 93.9 us (0.963)
  Pallas kernels: 96.5 us -> 92.7 us
    pallas_call x1, Pallas kernels: 91.1 us -> 87.2 us  [block(): pl.pallas_call(functools.partial(block_kernel, n, class_count), out_shape...]
where the time goes in v4:
time: 93.9 us; the launch traced here: 93.5 us
  Pallas kernels  92.7 us (99%)
    pallas_call x1, Pallas kernels, block(): pl.pallas_call(functools.partial(block_kernel, n, class_count), out_shape...  87.2 us
    pallas_call x1, Pallas kernels, tail(): pl.pallas_call(tail_kernel, out_shape=(jax.ShapeDtypeStruct((rows, tokens...  5.43 us

profile of v4, /device:TPU:0, one launch (start us, length us, event | category | flops | bytes accessed | tf_op | source)
XLA Modules:
  0.0 93.5 jit_solution(9506605095726173958)
XLA Ops:
  0.6 0.0 copy-start
  0.6 0.0 copy-start.1
  0.7 87.2 %shard_map.135 = (f32[128,1024]{1,0:T(8,128)S(1)}, f32[160,128]{1,0:T(8,128)S(1)}, bf16[160,1024]{1,0:T(8,128)(2,1)S(1)}, f32[1,128]{1,0:T(1,128)S(1)}, bf16[160...) custom-call(bf16[128,1024]{1,0:T(8,128)(2,1)} %x_ref.1, ...), custom_call_target="tpu_custom_call" | custom-call | tf_op jit(solution)/shard_map/pallas_call | solution.py:1063
  87.9 0.0 copy-done
  87.9 0.0 copy-done.1
  87.9 5.4 %shard_map.136 = (f32[128,1024]{1,0:T(8,128)}, f32[49,128]{1,0:T(8,128)}, f32[1,128]{1,0:T(1,128)}, f32[150,128]{1,0:T(8,128)}, f32[1,1]{1,0:T(1,128)}, /*index=5*/f32[512,2048]{1,0:T(8,128)}, f32[512,2048]{1,0:T(8,128)}) custom-call(bf16[128,1024]{1,0:T(8,128)(2,1)S(1)} %copy-done, f32[128,1024]{1,0:T(8,128)S(1)} %get-tuple-element.22.grad_ref, ...), custom_call_target="tpu_custom_call" | custom-call | tf_op jit(solution)/shard_map/pallas_call | solution.py:165
Async XLA Ops:
  0.6 87.3 %copy-start = (bf16[128,1024]{1,0:T(8,128)(2,1)S(1)}, bf16[128,1024]{1,0:T(8,128)(2,1)}, u32[]{:S(2)}) copy-start(bf16[128,1024]{1,0:T(8,128)(2,1)} %x_ref.1) | copy-start | bytes 786436
  0.6 87.3 %copy-start.1 = (f32[128,49]{0,1:T(8,128)S(1)}, f32[128,49]{0,1:T(8,128)}, u32[]{:S(2)}) copy-start(f32[128,49]{0,1:T(8,128)} %param.9) | copy-start | bytes 75268

commit v5 on v4

--- a/solution.py
+++ b/solution.py
@@ -232,7 +232,7 @@
     x_ref, taps_ref, gain_ref, scale_ref, labels_ref, head_ref, w_in_ref, w_out_ref, load_sem,
     x_grid, wide, taps, turned,
     conv_all, wg, wg_turned, acc, gains, stats, token_rows,
-    sh_high, sh_low, mix_high, mix_low, mix,
+    sh_high, sh_low, mix_both, mix,
     hidden, slope, narrow, back_rows, seen_narrow,
     tw_keep, tw_out, tw_in, rs_out, slots, packs,
     msg, t_in, y_out, y_in, u_in, d_in, z_out, sums,
@@ -377,8 +377,8 @@
     def mix_head():
         mixed = nt_dot(sh_high[...], w_out_ref[...]) + nt_dot(sh_low[...], w_out_ref[...])
         high = mixed.astype(jnp.bfloat16)
-        mix_high[...] = high
-        mix_low[...] = (mixed - high.astype(f32)).astype(jnp.bfloat16)
+        mix_both[0:classes, :] = high
+        mix_both[classes : 2 * classes, :] = (mixed - high.astype(f32)).astype(jnp.bfloat16)
 
     def mix_back():
         mix[...] = nt_dot(w_out_ref[...], sh_high[...]).astype(jnp.bfloat16)
@@ -554,35 +554,38 @@
         )
 
     def strip_at(d):
-        return lax.rem(base + d + 1, strips)
-
-    def activate(d):
-        j = strip_at(d)
-        own = lanes_of(j)
+        both = lax.rem(lax.div(base, 2) + d // 2 + 1, strips // 2)
+        side = lax.rem(base, 2)
+        return 2 * both + (side if d % 2 else 1 - side)
+
+    def activate(e):
+        j = lax.rem(lax.div(base, 2) + e + 1, strips // 2)
+        own = lanes_of(j, 2 * LANES)
         mean_here, inv_here = token_rows[0:1, own], token_rows[1:2, own]
 
         @pl.loop(0, units // chunk)
         def _(g):
             piece = rows_of(g, chunk)
-            pre = (acc[piece, own] - gains[piece, :] * mean_here) * inv_here
+            offset = jnp.concatenate([gains[piece, :]] * 2, axis=1)
+            pre = (acc[piece, own] - offset * mean_here) * inv_here
             cum_prob = 0.5 * (1.0 + lax.erf(pre * SQRT_HALF))
             density = jnp.exp(-0.5 * pre * pre) * NORMAL
             acc[piece, own] = pre
             hidden[piece, own] = (pre * cum_prob).astype(jnp.bfloat16)
             slope[piece, own] = (cum_prob + pre * density) * inv_here
 
-        active = hidden[:, own]
-        scores = (
-            nn_dot(mix_high[...], active)
-            + nn_dot(mix_low[...], active)
-            + nn_dot(own_scores[...], x_strip(own))
-        )
-        upper, lower = scores[0:pack], scores[pack : 2 * pack]
-        first = jnp.where(left, upper, pltpu.roll(lower, LANES // 2, 1))
-        second = jnp.where(left, pltpu.roll(upper, LANES // 2, 1), lower)
-        tw_keep[d] = jnp.where(c == 0, first, second)
-        tw_out[d] = jnp.where(c == 0, second, first)
-        to_twin_strip(d).start()
+        scores = nn_dot(mix_both[...], hidden[:, own])
+        scores = scores[0:classes] + scores[classes : 2 * classes] + nn_dot(own_scores[...], x_strip(own))
+        for side in range(2):
+            here = slice(side * LANES, (side + 1) * LANES)
+            upper, lower = scores[0:pack, here], scores[pack : 2 * pack, here]
+            first = jnp.where(left, upper, pltpu.roll(lower, LANES // 2, 1))
+            second = jnp.where(left, pltpu.roll(upper, LANES // 2, 1), lower)
+            d = 2 * e + jnp.where(lax.rem(base, 2) == side, 1, 0)
+            tw_keep[d] = jnp.where(c == 0, first, second)
+            tw_out[d] = jnp.where(c == 0, second, first)
+        for d in (2 * e, 2 * e + 1):
+            to_twin_strip(d).start()
 
     def pass_on(d):
         owner = strip_at(d) * step
@@ -601,10 +604,12 @@
     def x_strip(own):
         return x_ref[:, own] if rows == LANES else wide[:, own].astype(jnp.bfloat16)
 
-    for d in range(strips):
-        activate(d)
-        if d > 0:
-            pass_on(d - 1)
+    for e in range(strips // 2):
+        activate(e)
+        if e > 0:
+            pass_on(2 * e - 2)
+            pass_on(2 * e - 1)
+    pass_on(strips - 2)
     pass_on(strips - 1)
 
     def to_all(r):
@@ -770,7 +775,10 @@
                     block[:, core * rows : (core + 1) * rows], 1, LANES
                 )
 
-    slab = 32
+    def slabs(h):
+        low, high = cuts[h]
+        slab = max(k for k in range(16, 129, 16) if (high - low) % k == 0)
+        return [low + i * slab for i in range((high - low) // slab)], slab
 
     def sums_to_mate(h):
         return pltpu.make_async_remote_copy(
@@ -786,9 +794,9 @@
         to_twin(zz, 1 - y, c, h).wait_recv()
         low, high = cuts[h]
 
-        @pl.loop(low // slab, high // slab)
-        def _(g):
-            own = rows_of(g, slab)
+        starts, slab = slabs(h)
+        for start in starts:
+            own = slice(start, start + slab)
             y_out[k, own] = (
                 msg[index_of(zz, 1 - y, c), own].astype(f32)
                 + t_in[zz * 2 + 1 - y, own].astype(f32)
@@ -807,9 +815,9 @@
             def join():
                 sums_to_mate(h).wait_recv()
 
-                @pl.loop(low // slab, high // slab)
-                def _(g):
-                    own = rows_of(g, slab)
+                starts, slab = slabs(h)
+                for start in starts:
+                    own = slice(start, start + slab)
                     y_out[k, own] = (y_out[k, own].astype(f32) + m_in[own].astype(f32)).astype(
                         jnp.bfloat16
                     )
@@ -858,18 +866,18 @@
     def sum_up(zz, h, with_across):
         low, high = cuts[h]
 
-        @pl.loop(low // slab, high // slab)
-        def _(g):
-            own = rows_of(g, slab)
+        starts, slab = slabs(h)
+        for start in starts:
+            own = slice(start, start + slab)
             total = msg[index_of(zz, y, c), own].astype(f32) + t_in[zz * 2 + y, own].astype(f32)
             sums[own] = total + y_in[zz, own].astype(f32) if with_across else total
 
     def add(landing, zz, h):
         low, high = cuts[h]
 
-        @pl.loop(low // slab, high // slab)
-        def _(g):
-            own = rows_of(g, slab)
+        starts, slab = slabs(h)
+        for start in starts:
+            own = slice(start, start + slab)
             sums[own] += landing[zz, own].astype(f32)
 
     for i, (k, h) in enumerate(turns):
@@ -1024,8 +1032,7 @@
         pltpu.VMEM((SUB, tokens), f32),
         pltpu.VMEM((classes, channels), bf16),
         pltpu.VMEM((classes, channels), bf16),
-        pltpu.VMEM((classes, units), bf16),
-        pltpu.VMEM((classes, units), bf16),
+        pltpu.VMEM((2 * classes, units), bf16),
         pltpu.VMEM((units, classes), bf16),
         pltpu.VMEM((units, tokens), bf16),
         pltpu.VMEM((units, tokens), f32),

time: 93.9 us -> 93.1 us (level)
  no operation moved by 1% of the time
where the time goes in v5:
time: 93.1 us; the launch traced here: 93 us
  Pallas kernels  92.1 us (99%)
    pallas_call x1, Pallas kernels, block(): pl.pallas_call(functools.partial(block_kernel, n, class_count), out_shape...  86.7 us
    pallas_call x1, Pallas kernels, tail(): pl.pallas_call(tail_kernel, out_shape=(jax.ShapeDtypeStruct((rows, tokens...  5.44 us

profile of v5, /device:TPU:0, one launch (start us, length us, event | category | flops | bytes accessed | tf_op | source)
XLA Modules:
  0.0 93.0 jit_solution(6971886325116115988)
XLA Ops:
  0.6 0.0 copy-start
  0.6 0.0 copy-start.1
  0.7 86.7 %shard_map.135 = (f32[128,1024]{1,0:T(8,128)S(1)}, f32[160,128]{1,0:T(8,128)S(1)}, bf16[160,1024]{1,0:T(8,128)(2,1)S(1)}, f32[1,128]{1,0:T(1,128)S(1)}, bf16[160...) custom-call(bf16[128,1024]{1,0:T(8,128)(2,1)} %x_ref.1, ...), custom_call_target="tpu_custom_call" | custom-call | tf_op jit(solution)/shard_map/pallas_call | solution.py:1070
  87.3 0.0 copy-done
  87.3 0.0 copy-done.1
  87.4 5.4 %shard_map.136 = (f32[128,1024]{1,0:T(8,128)}, f32[49,128]{1,0:T(8,128)}, f32[1,128]{1,0:T(1,128)}, f32[150,128]{1,0:T(8,128)}, f32[1,1]{1,0:T(1,128)}, /*index=5*/f32[512,2048]{1,0:T(8,128)}, f32[512,2048]{1,0:T(8,128)}) custom-call(bf16[128,1024]{1,0:T(8,128)(2,1)S(1)} %copy-done, f32[128,1024]{1,0:T(8,128)S(1)} %get-tuple-element.22.grad_ref, ...), custom_call_target="tpu_custom_call" | custom-call | tf_op jit(solution)/shard_map/pallas_call | solution.py:165
Async XLA Ops:
  0.6 86.7 %copy-start = (bf16[128,1024]{1,0:T(8,128)(2,1)S(1)}, bf16[128,1024]{1,0:T(8,128)(2,1)}, u32[]{:S(2)}) copy-start(bf16[128,1024]{1,0:T(8,128)(2,1)} %x_ref.1) | copy-start | bytes 786436
  0.6 86.7 %copy-start.1 = (f32[128,49]{0,1:T(8,128)S(1)}, f32[128,49]{0,1:T(8,128)}, u32[]{:S(2)}) copy-start(f32[128,49]{0,1:T(8,128)} %param.9) | copy-start | bytes 75268

commit v6 on v5

--- a/solution.py
+++ b/solution.py
@@ -356,13 +356,22 @@
     pair = 2 * rows
     gains[...] = jnp.zeros_like(gains)
     ones = jnp.ones((pair, LANES), jnp.bfloat16)
-    for p in range(m):
+
+    def weigh(p):
         own = slice(p * pair, (p + 1) * pair)
         gained = w_in_ref[:, own].astype(f32) * gain_ref[:, own]
         gained_narrow = gained.astype(jnp.bfloat16)
         wg[p] = gained_narrow
         wg_turned[p] = gained.T.astype(jnp.bfloat16)
         gains[...] += nn_dot(gained_narrow, ones)
+
+    soon = m // 2 if balance else m
+    for p in range(soon):
+        weigh(p)
+
+    def weigh_rest():
+        for p in range(soon, m):
+            weigh(p)
 
     def scale_head():
         for load in loads[4:]:
@@ -482,9 +491,9 @@
                 absorb((2 * z - mate) * 2 + 1 - y)
 
     work = {
-        (1, 0): [scale_head],
-        (1, 1): [mix_head],
-        (2, 0): [mix_back],
+        (1, 0): [weigh_rest],
+        (1, 1): [scale_head],
+        (2, 0): [mix_head, mix_back],
         (2, 1): [lambda: absorb_at(0, y), lambda: absorb_at(0, 1 - y)],
         (3, 0): [lambda: absorb_at(1, y)],
         (3, 1): [lambda: absorb_at(2, y), lambda: absorb_beside(True)],

time: 93.1 us -> 94.4 us (1.014)
  Pallas kernels: 92.1 us -> 93.3 us
    pallas_call x1, Pallas kernels: 86.7 us -> 87.9 us  [block(): pl.pallas_call(functools.partial(block_kernel, n, class_count), out_shape...]
where the time goes in v6:
time: 94.4 us; the launch traced here: 94.2 us
  Pallas kernels  93.3 us (99%)
    pallas_call x1, Pallas kernels, block(): pl.pallas_call(functools.partial(block_kernel, n, class_count), out_shape...  87.9 us
    pallas_call x1, Pallas kernels, tail(): pl.pallas_call(tail_kernel, out_shape=(jax.ShapeDtypeStruct((rows, tokens...  5.44 us

profile of v6, /device:TPU:0, one launch (start us, length us, event | category | flops | bytes accessed | tf_op | source)
XLA Modules:
  0.0 94.2 jit_solution(183265629493153347)
XLA Ops:
  0.6 0.0 copy-start
  0.6 0.0 copy-start.1
  0.7 87.9 %shard_map.135 = (f32[128,1024]{1,0:T(8,128)S(1)}, f32[160,128]{1,0:T(8,128)S(1)}, bf16[160,1024]{1,0:T(8,128)(2,1)S(1)}, f32[1,128]{1,0:T(1,128)S(1)}, bf16[160...) custom-call(bf16[128,1024]{1,0:T(8,128)(2,1)} %x_ref.1, ...), custom_call_target="tpu_custom_call" | custom-call | tf_op jit(solution)/shard_map/pallas_call | solution.py:1079
  88.6 0.0 copy-done
  88.6 0.0 copy-done.1
  88.6 5.4 %shard_map.136 = (f32[128,1024]{1,0:T(8,128)}, f32[49,128]{1,0:T(8,128)}, f32[1,128]{1,0:T(1,128)}, f32[150,128]{1,0:T(8,128)}, f32[1,1]{1,0:T(1,128)}, /*index=5*/f32[512,2048]{1,0:T(8,128)}, f32[512,2048]{1,0:T(8,128)}) custom-call(bf16[128,1024]{1,0:T(8,128)(2,1)S(1)} %copy-done, f32[128,1024]{1,0:T(8,128)S(1)} %get-tuple-element.22.grad_ref, ...), custom_call_target="tpu_custom_call" | custom-call | tf_op jit(solution)/shard_map/pallas_call | solution.py:165
Async XLA Ops:
  0.6 87.9 %copy-start = (bf16[128,1024]{1,0:T(8,128)(2,1)S(1)}, bf16[128,1024]{1,0:T(8,128)(2,1)}, u32[]{:S(2)}) copy-start(bf16[128,1024]{1,0:T(8,128)(2,1)} %x_ref.1) | copy-start | bytes 786436
  0.6 87.9 %copy-start.1 = (f32[128,49]{0,1:T(8,128)S(1)}, f32[128,49]{0,1:T(8,128)}, u32[]{:S(2)}) copy-start(f32[128,49]{0,1:T(8,128)} %param.9) | copy-start | bytes 75268
